TPU v7x, 512 devices: a whole 4x8x8 slice. The times are simulated.
512 devices in a mesh: gy: 16 (over y, core), gz: 32 (over x, z).
Axes of the slice: x: 4, y: 8, z: 8, core: 2. Of those that a mesh axis runs over, the one named last changes fastest.
Arguments:
- electric_level: float32 [256, 256, 128], P('gz', 'gy'), may hold values from -3 to 3
- impurity_atoms: int32 [256, 256, 128], P('gz', 'gy'), may hold values from 0 to 11
- cell_materials: int32 [256, 256, 128], P('gz', 'gy'), may hold values from 0 to 2, as said below
Outputs:
- updated: float32 [256, 256, 128], P('gz', 'gy')
Inputs may be any that keep to these rules, and one draw needn't show every extreme that they name: `cell_materials`: material ids; the cells of one z line that are not silicon (0) all hold one material.
All inputs are finite; a program needn't handle non-finite values.
Results may differ from a plain program's by a relative error of at most 0.0015.
Values sent between devices are 32-bit elements; how exact they have to be, the bound alone decides.
A program may use at most 64 MiB of HBM per device.

v0:
```python
from functools import reduce

import jax
import jax.numpy as jnp
from jax import lax
from jax.sharding import PartitionSpec as P

ZW = 8192


def prefix_2(value, axis, join, neutral, backward):
    count, mine = (lax.axis_size(axis), lax.axis_index(axis))
    pieces = jax.tree.map(lambda part: lax.all_gather(part, axis), value)
    if backward:
        pieces = jax.tree.map(lambda part: part[::-1], pieces)
        mine = count - 1 - mine
    running = jax.tree.map(
        lambda part, zero: jnp.full_like(part, 0) + jnp.asarray(zero, part.dtype), value, neutral
    )

    def turn(position, running):
        longer = join(running, jax.tree.map(lambda part: part[position], pieces))
        return jax.tree.map(lambda new, old: jnp.where(position < mine, new, old), longer, running)

    return lax.fori_loop(0, count - 1, turn, running)


def with_halo(cells, sides, width):
    for axis, dim in sides:
        count = lax.axis_size(axis)
        ends = count - 1
        head = lax.slice_in_dim(cells, 0, width, axis=dim)
        tail = lax.slice_in_dim(cells, cells.shape[dim] - width, cells.shape[dim], axis=dim)
        cells = jnp.concatenate(
            [
                lax.ppermute(tail, axis, [(i, (i + 1) % count) for i in range(ends)]),
                cells,
                lax.ppermute(head, axis, [((i + 1) % count, i) for i in range(ends)]),
            ],
            axis=dim,
        )
    return cells


def harmonic(own, other):
    other_fill = jnp.where(other > 0, other, own)
    return 2.0 * own * other_fill / (own + other_fill)


def beside_all(padded):
    centre = padded[1:-1, 1:-1]
    return (
        padded[:-2, 1:-1],
        padded[2:, 1:-1],
        padded[1:-1, :-2],
        padded[1:-1, 2:],
        jnp.pad(centre[:, :, :-1], ((0, 0), (0, 0), (1, 0))),
        jnp.pad(centre[:, :, 1:], ((0, 0), (0, 0), (0, 1))),
    )


def compose(earlier, later):
    l00, l01, l10, l11, lu0, lu1, lvv = later
    e00, e01, e10, e11, eu0, eu1, evv = earlier
    merged = (
        l00 * e00 + l01 * e10,
        l00 * e01 + l01 * e11,
        l10 * e00 + l11 * e10,
        l10 * e01 + l11 * e11,
        lu0 * e00 + lu1 * e10 + lvv * eu0,
        lu0 * e01 + lu1 * e11 + lvv * eu1,
        lvv * evv,
    )
    scale = reduce(jnp.maximum, [jnp.abs(entry) for entry in merged])
    return tuple((entry / scale for entry in merged))


def chain_back(earlier, later):
    return (later[0] * earlier[0], later[0] * earlier[1] + later[1])


def solve_lines(lower, principal_entries, upper, rhs):
    zeros = jnp.zeros_like(rhs)
    ones = jnp.ones_like(rhs[0])
    flats = jnp.zeros_like(rhs[0])
    elements = (zeros, upper, -lower, principal_entries, zeros, rhs, -lower)
    prefix = lax.associative_scan(compose, elements, axis=0)
    total = tuple((entry[-1] for entry in prefix))
    identity = (ones, flats, flats, ones, flats, flats, ones)
    before = prefix_2(total, "gz", compose, identity, False)
    start_p, start_q, start_r = (before[1], before[3], before[5])
    prod_p = prefix[0] * start_p + prefix[1] * start_q
    prod_q = prefix[2] * start_p + prefix[3] * start_q
    prod_r = prefix[4] * start_p + prefix[5] * start_q + prefix[6] * start_r
    ratio_c = prod_p / prod_q
    ratio_d = prod_r / prod_q
    back = lax.associative_scan(chain_back, (-ratio_c, ratio_d), reverse=True, axis=0)
    after = prefix_2((back[0][0], back[1][0]), "gz", chain_back, (ones, flats), True)
    ending = after[1]
    return back[0] * ending + back[1]


def line_solve(lower, principal_entries, upper, rhs):
    return solve_lines(lower, principal_entries, upper, rhs)


def colour_lines(field, colour):
    depth, rows, cols = field.shape
    paired = field.reshape(depth, rows, cols // 2, 2)
    parity = (jnp.arange(rows) % 2)[None, :, None]
    chosen = jnp.where(parity == colour, paired[..., 0], paired[..., 1])
    return chosen.reshape(depth, -1)


def colour_field(values, colour, shape):
    depth, rows, cols = shape
    shaped = values.reshape(depth, rows, cols // 2)
    parity = (jnp.arange(rows) % 2)[None, :, None]
    even_part = jnp.where(parity == colour, shaped, 0.0)
    odd_part = jnp.where(parity == colour, 0.0, shaped)
    return jnp.stack([even_part, odd_part], axis=-1).reshape(depth, rows, cols)


def block_sum(field):
    depth, rows, cols = field.shape
    return field.reshape(depth, rows // 2, 2, cols // 2, 2).sum(axis=(2, 4))


def body(electric_level, impurity_atoms, cell_materials):
    depth, rows, cols = electric_level.shape
    z_weight = ZW * 1.0
    permit = jnp.where(cell_materials == 0, 1.0, jnp.where(cell_materials == 1, 0.33, 0.64)).astype(
        jnp.float32
    )
    electron_population = (cell_materials == 0).astype(jnp.float32)
    volume_ionic_excess = electron_population * (0.5 * impurity_atoms.astype(jnp.float32) - 1.5)
    rims = (
        with_halo(electric_level, (("gy", 1), ("gz", 0)), 1),
        with_halo(permit, (("gy", 1), ("gz", 0)), 1),
    )
    near_pot = beside_all(rims[0])
    near_perm = beside_all(rims[1])
    weights = (z_weight, z_weight, 1.0, 1.0, 1.0, 1.0)
    faces = [weight_val * harmonic(permit, other) for weight_val, other in zip(weights, near_perm)]
    neighbour_link_total = faces[0] + faces[1] + faces[2] + faces[3] + faces[4] + faces[5]
    collected_entries = faces[0] * near_pot[0]
    for index in range(1, 6):
        collected_entries = collected_entries + faces[index] * near_pot[index]
    source_vector = (
        neighbour_link_total * electric_level
        - collected_entries
        + electron_population * 2.0 * jnp.sinh(electric_level)
        - volume_ionic_excess
    )
    rhs = -source_vector
    principal_entries = neighbour_link_total + electron_population * 2.0 * jnp.cosh(electric_level)
    lower = jnp.where(near_perm[0] > 0, -faces[0], 0.0)
    upper = jnp.where(near_perm[1] > 0, -faces[1], 0.0)
    lines_low = [colour_lines(lower, colour) for colour in (0, 1)]
    lines_diag = [colour_lines(principal_entries, colour) for colour in (0, 1)]
    lines_up = [colour_lines(upper, colour) for colour in (0, 1)]
    first_lines = line_solve(lines_low[0], lines_diag[0], lines_up[0], colour_lines(rhs, 0))
    first = colour_field(first_lines, 0, electric_level.shape)
    sides = with_halo(first, (("gy", 1),), 1)
    near_first = beside_all(jnp.pad(sides, ((1, 1), (0, 0), (0, 0))))
    side = (
        faces[2] * near_first[2]
        + faces[3] * near_first[3]
        + faces[4] * near_first[4]
        + faces[5] * near_first[5]
    )
    second_lines = line_solve(lines_low[1], lines_diag[1], lines_up[1], colour_lines(rhs + side, 1))
    delta = first + colour_field(second_lines, 1, electric_level.shape)
    near_delta = beside_all(with_halo(delta, (("gy", 1), ("gz", 0)), 1))
    applied = principal_entries * delta
    for index in range(6):
        applied = applied - faces[index] * near_delta[index]
    resid = rhs - applied
    x_inner = faces[5][:, :, 0::2].reshape(depth, rows // 2, 2, cols // 2).sum(axis=2)
    y_inner = faces[3][:, 0::2, :].reshape(depth, rows // 2, cols // 2, 2).sum(axis=3)
    coarse_diag = block_sum(principal_entries) - 2.0 * (x_inner + y_inner)
    coarse_lines = line_solve(
        block_sum(lower).reshape(depth, -1),
        coarse_diag.reshape(depth, -1),
        block_sum(upper).reshape(depth, -1),
        block_sum(resid).reshape(depth, -1),
    )
    coarse = coarse_lines.reshape(depth, rows // 2, cols // 2)
    spread = jnp.repeat(jnp.repeat(coarse, 2, axis=1), 2, axis=2)
    return electric_level + delta + spread


def solution(mesh):
    placed = (P("gz", "gy", None), P("gz", "gy", None), P("gz", "gy", None))
    return jax.shard_map(
        body, mesh=mesh, in_specs=placed, out_specs=P("gz", "gy", None), check_vma=False
    )
```

profile of v0, /device:TPU:32, one launch (start us, length us, event | category | flops | bytes accessed | tf_op | source)
XLA Modules:
  0.0 1317.4 jit_solution(16352765407564971130)
XLA Ops:
  0.9 1.9 collective-permute-start
  2.8 4.9 collective-permute-start.1
  7.7 1.9 collective-permute-start.4
  9.6 4.9 collective-permute-start.5
  14.7 1.3 collective-permute-start.2
  16.0 4.9 collective-permute-start.3
  20.9 4.4 collective-permute-start.6
  25.4 1.3 collective-permute-start.7
  28.8 2.5 collective-permute-done.7
  42.0 50.5 %all-gather.6 = f32[32,1,1024]{2,1,0:T(1,128)S(1)} all-gather(f32[1,1,1024]{2,1,0:T(1,128)S(1)} %add_bitcast_fusion.11), channel_id=1, replica_groups=mesh['gy'=16,'gz'=32] {'gz'}, dimensions={0}, use_global_device_ids=true | all-gather | bytes 135168 | tf_op jit(solution)/shard_map/all_gather | solution.py:13
  94.2 41.1 %all-gather.5 = f32[32,1,1024]{2,1,0:T(1,128)S(1)} all-gather(f32[1,1,1024]{2,1,0:T(1,128)S(1)} %add_bitcast_fusion.12), channel_id=1, replica_groups=mesh['gy'=16,'gz'=32] {'gz'}, dimensions={0}, use_global_device_ids=true | all-gather | bytes 135168 | tf_op jit(solution)/shard_map/all_gather | solution.py:13
  135.3 42.1 %all-gather.4 = f32[32,1,1024]{2,1,0:T(1,128)S(1)} all-gather(f32[1,1,1024]{2,1,0:T(1,128)S(1)} %add_bitcast_fusion.13), channel_id=1, replica_groups=mesh['gy'=16,'gz'=32] {'gz'}, dimensions={0}, use_global_device_ids=true | all-gather | bytes 135168 | tf_op jit(solution)/shard_map/all_gather | solution.py:13
  177.7 41.0 %all-gather.3 = f32[32,1,1024]{2,1,0:T(1,128)S(1)} all-gather(f32[1,1,1024]{2,1,0:T(1,128)S(1)} %add_bitcast_fusion.14), channel_id=1, replica_groups=mesh['gy'=16,'gz'=32] {'gz'}, dimensions={0}, use_global_device_ids=true | all-gather | bytes 135168 | tf_op jit(solution)/shard_map/all_gather | solution.py:13
  218.8 42.1 %all-gather.2 = f32[32,1,1024]{2,1,0:T(1,128)S(1)} all-gather(f32[1,1,1024]{2,1,0:T(1,128)S(1)} %add_bitcast_fusion.15), channel_id=1, replica_groups=mesh['gy'=16,'gz'=32] {'gz'}, dimensions={0}, use_global_device_ids=true | all-gather | bytes 135168 | tf_op jit(solution)/shard_map/all_gather | solution.py:13
  261.2 41.0 %all-gather.1 = f32[32,1,1024]{2,1,0:T(1,128)S(1)} all-gather(f32[1,1,1024]{2,1,0:T(1,128)S(1)} %add_bitcast_fusion.16), channel_id=1, replica_groups=mesh['gy'=16,'gz'=32] {'gz'}, dimensions={0}, use_global_device_ids=true | all-gather | bytes 135168 | tf_op jit(solution)/shard_map/all_gather | solution.py:13
  302.3 42.1 %all-gather = f32[32,1,1024]{2,1,0:T(1,128)S(1)} all-gather(f32[1,1,1024]{2,1,0:T(1,128)S(1)} %add_bitcast_fusion.17), channel_id=1, replica_groups=mesh['gy'=16,'gz'=32] {'gz'}, dimensions={0}, use_global_device_ids=true | all-gather | bytes 135168 | tf_op jit(solution)/shard_map/all_gather | solution.py:13
  345.1 5.2 while.120
  352.6 41.0 %all-gather.8 = f32[32,1,1024]{2,1,0:T(1,128)S(1)} all-gather(f32[1,1,1024]{2,1,0:T(1,128)S(1)} %add_bitcast_fusion.9), channel_id=1, replica_groups=mesh['gy'=16,'gz'=32] {'gz'}, dimensions={0}, use_global_device_ids=true | all-gather | bytes 135168 | tf_op jit(solution)/shard_map/all_gather | solution.py:13
  393.7 42.3 %all-gather.7 = f32[32,1,1024]{2,1,0:T(1,128)S(1)} all-gather(f32[1,1,1024]{2,1,0:T(1,128)S(1)} %add_bitcast_fusion.10), channel_id=1, replica_groups=mesh['gy'=16,'gz'=32] {'gz'}, dimensions={0}, use_global_device_ids=true | all-gather | bytes 135168 | tf_op jit(solution)/shard_map/all_gather | solution.py:13
  436.7 1.8 while.121
  443.9 1.9 collective-permute-start.8
  445.8 4.9 collective-permute-start.9
  462.8 41.0 %all-gather.15 = f32[32,1,1024]{2,1,0:T(1,128)S(1)} all-gather(f32[1,1,1024]{2,1,0:T(1,128)S(1)} %add_bitcast_fusion.2), channel_id=1, replica_groups=mesh['gy'=16,'gz'=32] {'gz'}, dimensions={0}, use_global_device_ids=true | all-gather | bytes 135168 | tf_op jit(solution)/shard_map/all_gather | solution.py:13
  504.7 42.1 %all-gather.14 = f32[32,1,1024]{2,1,0:T(1,128)S(1)} all-gather(f32[1,1,1024]{2,1,0:T(1,128)S(1)} %add_bitcast_fusion.3), channel_id=1, replica_groups=mesh['gy'=16,'gz'=32] {'gz'}, dimensions={0}, use_global_device_ids=true | all-gather | bytes 135168 | tf_op jit(solution)/shard_map/all_gather | solution.py:13
  547.0 41.1 %all-gather.13 = f32[32,1,1024]{2,1,0:T(1,128)S(1)} all-gather(f32[1,1,1024]{2,1,0:T(1,128)S(1)} %add_bitcast_fusion.4), channel_id=1, replica_groups=mesh['gy'=16,'gz'=32] {'gz'}, dimensions={0}, use_global_device_ids=true | all-gather | bytes 135168 | tf_op jit(solution)/shard_map/all_gather | solution.py:13
  588.1 42.0 %all-gather.12 = f32[32,1,1024]{2,1,0:T(1,128)S(1)} all-gather(f32[1,1,1024]{2,1,0:T(1,128)S(1)} %add_bitcast_fusion.5), channel_id=1, replica_groups=mesh['gy'=16,'gz'=32] {'gz'}, dimensions={0}, use_global_device_ids=true | all-gather | bytes 135168 | tf_op jit(solution)/shard_map/all_gather | solution.py:13
  630.3 41.1 %all-gather.11 = f32[32,1,1024]{2,1,0:T(1,128)S(1)} all-gather(f32[1,1,1024]{2,1,0:T(1,128)S(1)} %add_bitcast_fusion.6), channel_id=1, replica_groups=mesh['gy'=16,'gz'=32] {'gz'}, dimensions={0}, use_global_device_ids=true | all-gather | bytes 135168 | tf_op jit(solution)/shard_map/all_gather | solution.py:13
  672.1 42.1 %all-gather.10 = f32[32,1,1024]{2,1,0:T(1,128)S(1)} all-gather(f32[1,1,1024]{2,1,0:T(1,128)S(1)} %add_bitcast_fusion.7), channel_id=1, replica_groups=mesh['gy'=16,'gz'=32] {'gz'}, dimensions={0}, use_global_device_ids=true | all-gather | bytes 135168 | tf_op jit(solution)/shard_map/all_gather | solution.py:13
  714.3 41.3 %all-gather.9 = f32[32,1,1024]{2,1,0:T(1,128)S(1)} all-gather(f32[1,1,1024]{2,1,0:T(1,128)S(1)} %add_bitcast_fusion.8), channel_id=1, replica_groups=mesh['gy'=16,'gz'=32] {'gz'}, dimensions={0}, use_global_device_ids=true | all-gather | bytes 135168 | tf_op jit(solution)/shard_map/all_gather | solution.py:13
  756.3 5.2 while.122
  763.8 42.0 %all-gather.17 = f32[32,1,1024]{2,1,0:T(1,128)S(1)} all-gather(f32[1,1,1024]{2,1,0:T(1,128)S(1)} %add_bitcast_fusion), channel_id=1, replica_groups=mesh['gy'=16,'gz'=32] {'gz'}, dimensions={0}, use_global_device_ids=true | all-gather | bytes 135168 | tf_op jit(solution)/shard_map/all_gather | solution.py:13
  806.1 41.1 %all-gather.16 = f32[32,1,1024]{2,1,0:T(1,128)S(1)} all-gather(f32[1,1,1024]{2,1,0:T(1,128)S(1)} %add_bitcast_fusion.1), channel_id=1, replica_groups=mesh['gy'=16,'gz'=32] {'gz'}, dimensions={0}, use_global_device_ids=true | all-gather | bytes 135168 | tf_op jit(solution)/shard_map/all_gather | solution.py:13
  847.8 1.8 while.123
  850.7 1.9 collective-permute-start.10
  852.6 4.9 collective-permute-start.11
  864.6 2.8 collective-permute-start.12
  868.8 4.2 collective-permute-done.13
  878.6 50.3 %all-gather.24 = f32[32,1,512]{2,1,0:T(1,128)S(1)} all-gather(f32[1,1,512]{2,1,0:T(1,128)S(1)} %add_bitcast_fusion.20), channel_id=1, replica_groups=mesh['gy'=16,'gz'=32] {'gz'}, dimensions={0}, use_global_device_ids=true | all-gather | bytes 67584 | tf_op jit(solution)/shard_map/all_gather | solution.py:13
  929.1 46.0 %all-gather.23 = f32[32,1,512]{2,1,0:T(1,128)S(1)} all-gather(f32[1,1,512]{2,1,0:T(1,128)S(1)} %add_bitcast_fusion.21), channel_id=1, replica_groups=mesh['gy'=16,'gz'=32] {'gz'}, dimensions={0}, use_global_device_ids=true | all-gather | bytes 67584 | tf_op jit(solution)/shard_map/all_gather | solution.py:13
  975.1 48.2 %all-gather.22 = f32[32,1,512]{2,1,0:T(1,128)S(1)} all-gather(f32[1,1,512]{2,1,0:T(1,128)S(1)} %add_bitcast_fusion.22), channel_id=1, replica_groups=mesh['gy'=16,'gz'=32] {'gz'}, dimensions={0}, use_global_device_ids=true | all-gather | bytes 67584 | tf_op jit(solution)/shard_map/all_gather | solution.py:13
  1023.4 46.0 %all-gather.21 = f32[32,1,512]{2,1,0:T(1,128)S(1)} all-gather(f32[1,1,512]{2,1,0:T(1,128)S(1)} %add_bitcast_fusion.23), channel_id=1, replica_groups=mesh['gy'=16,'gz'=32] {'gz'}, dimensions={0}, use_global_device_ids=true | all-gather | bytes 67584 | tf_op jit(solution)/shard_map/all_gather | solution.py:13
  1069.5 48.2 %all-gather.20 = f32[32,1,512]{2,1,0:T(1,128)S(1)} all-gather(f32[1,1,512]{2,1,0:T(1,128)S(1)} %add_bitcast_fusion.24), channel_id=1, replica_groups=mesh['gy'=16,'gz'=32] {'gz'}, dimensions={0}, use_global_device_ids=true | all-gather | bytes 67584 | tf_op jit(solution)/shard_map/all_gather | solution.py:13
  1117.7 46.0 %all-gather.19 = f32[32,1,512]{2,1,0:T(1,128)S(1)} all-gather(f32[1,1,512]{2,1,0:T(1,128)S(1)} %add_bitcast_fusion.25), channel_id=1, replica_groups=mesh['gy'=16,'gz'=32] {'gz'}, dimensions={0}, use_global_device_ids=true | all-gather | bytes 67584 | tf_op jit(solution)/shard_map/all_gather | solution.py:13
  1163.8 48.2 %all-gather.18 = f32[32,1,512]{2,1,0:T(1,128)S(1)} all-gather(f32[1,1,512]{2,1,0:T(1,128)S(1)} %add_bitcast_fusion.26), channel_id=1, replica_groups=mesh['gy'=16,'gz'=32] {'gz'}, dimensions={0}, use_global_device_ids=true | all-gather | bytes 67584 | tf_op jit(solution)/shard_map/all_gather | solution.py:13
  1212.7 5.0 while.124
  1219.3 46.0 %all-gather.26 = f32[32,1,512]{2,1,0:T(1,128)S(1)} all-gather(f32[1,1,512]{2,1,0:T(1,128)S(1)} %add_bitcast_fusion.18), channel_id=1, replica_groups=mesh['gy'=16,'gz'=32] {'gz'}, dimensions={0}, use_global_device_ids=true | all-gather | bytes 67584 | tf_op jit(solution)/shard_map/all_gather | solution.py:13
  1265.4 48.2 %all-gather.25 = f32[32,1,512]{2,1,0:T(1,128)S(1)} all-gather(f32[1,1,512]{2,1,0:T(1,128)S(1)} %add_bitcast_fusion.19), channel_id=1, replica_groups=mesh['gy'=16,'gz'=32] {'gz'}, dimensions={0}, use_global_device_ids=true | all-gather | bytes 67584 | tf_op jit(solution)/shard_map/all_gather | solution.py:13
  1314.3 1.7 while.125
  (1483 shorter events, 72.1 us)
Async XLA Ops:
  0.0 7.7 copy-start
  0.9 13.7 %collective-permute-start = (f32[8,1,128]{2,1,0:T(1,128)S(1)}, f32[8,1,128]{2,1,0:T(1,128)S(1)}, u32[]{:S(2)}, u32[]{:S(2)}) collective-permute-start(f32[8,1,128]{2,1,0:T(1,128)S(1)} %get-tuple-element.1652), channel_id=1, source_target_pairs={{0,32},{32,64},{64,96},{96,128},{128,160},{160,192},{192,224},{224... | collective-permute-start | bytes 12296 | tf_op jit(solution)/shard_map/ppermute | solution.py:36
  2.8 11.8 collective-permute-start.1
  7.7 13.2 collective-permute-start.4
  9.6 11.2 collective-permute-start.5
  14.6 21.1 %copy-start.10 = (f32[8,1,128]{2,1,0:T(1,128)}, f32[8,1,128]{2,1,0:T(1,128)S(1)}, u32[]{:S(2)}) copy-start(f32[8,1,128]{2,1,0:T(1,128)S(1)} %collective-permute-done) | copy-start | bytes 12292
  14.6 21.1 %copy-start.24 = (f32[8,1,128]{2,1,0:T(1,128)}, f32[8,1,128]{2,1,0:T(1,128)S(1)}, u32[]{:S(2)}) copy-start(f32[8,1,128]{2,1,0:T(1,128)S(1)} %collective-permute-done.1) | copy-start | bytes 12292
  14.7 14.1 %collective-permute-start.2 = (f32[1,18,128]{2,1,0:T(8,128)S(1)}, f32[1,18,128]{2,1,0:T(8,128)S(1)}, u32[]{:S(2)}, u32[]{:S(2)}) collective-permute-start(f32[1,18,128]{2,1,0:T(8,128)S(1)} %get-tuple-element.1626), channel_id=1, source_target_pairs={{1,0},{2,1},{3,2},{4,3},{5,4},{6,5},{7,6},{8,7},{9,8},{10,9},{11,1... | collective-permute-start | bytes 27656 | tf_op jit(solution)/shard_map/ppermute | solution.py:38
  16.0 12.8 collective-permute-start.3
  20.9 10.4 copy-start.29
  20.9 10.4 copy-start.1
  20.9 7.8 collective-permute-start.6
  25.4 6.0 collective-permute-start.7
  26.7 1.3 copy-start.38
  28.8 7.0 copy-start.5
  28.8 7.0 copy-start.7
  38.3 0.8 copy-start.21
  38.3 0.8 copy-start.22
  38.3 0.8 copy-start.23
  38.3 0.8 copy-start.33
  38.3 0.8 copy-start.41
  38.5 0.8 copy-start.18
  38.5 0.8 copy-start.19
  38.5 0.8 copy-start.20
  344.4 0.7 copy-start.27
  443.9 14.8 %collective-permute-start.8 = (f32[8,1,128]{2,1,0:T(1,128)}, f32[8,1,128]{2,1,0:T(1,128)}, u32[]{:S(2)}, u32[]{:S(2)}) collective-permute-start(f32[8,1,128]{2,1,0:T(1,128)} %get-tuple-element.1640), channel_id=1, source_target_pairs={{0,32},{32,64},{64,96},{96,128},{128,160},{160,192},{192,224},{224... | collective-permute-start | bytes 12296 | tf_op jit(solution)/shard_map/ppermute | solution.py:36
  445.8 12.8 collective-permute-start.9
  451.5 0.8 copy-start.15
  454.3 0.8 copy-start.4
  455.1 0.8 copy-start.3
  455.9 0.8 copy-start.17
  456.3 0.8 copy-start.16
  457.8 0.9 copy-start.2
  457.8 0.9 copy-start.11
  460.2 0.7 copy-start.34
  503.8 0.7 copy-start.37
  671.3 0.7 copy-start.32
  847.2 0.7 copy-start.13
  850.7 13.9 %collective-permute-start.10 = (f32[8,1,128]{2,1,0:T(1,128)S(1)}, f32[8,1,128]{2,1,0:T(1,128)S(1)}, u32[]{:S(2)}, u32[]{:S(2)}) collective-permute-start(f32[8,1,128]{2,1,0:T(1,128)S(1)} %get-tuple-element.1634), channel_id=1, source_target_pairs={{0,32},{32,64},{64,96},{96,128},{128,160},{160,192},{192,224},{224... | collective-permute-start | bytes 12296 | tf_op jit(solution)/shard_map/ppermute | solution.py:36
  852.6 5.0 copy-start.9
  852.6 11.9 collective-permute-start.11
  863.1 0.7 copy-start.31
  864.6 4.2 collective-permute-start.12
  867.4 5.6 collective-permute-start.13
  868.7 4.3 copy-start.6
  868.7 4.3 copy-start.8
  868.7 4.3 copy-start.12
  868.7 4.3 copy-start.25
  (9 other events, 5.9 us)
where the time goes:
time: 1320 us
  blocking collectives  1180 us (89%)
  local copies, waits for them, and re-layouts  54.2 us (4%)
  starting transfers between devices  43.1 us (3%)
  other arithmetic  16.6 us (1%)
    all_gather x27, blocking collectives, prefix_2(): pieces = jax.tree.map(lambda part: lax.all_gather(part, axis), value)  1180 us
  transfers between devices with their start and end apart: 14, of which 2 were waited for; matrix products, arithmetic and copies ran while one was open for 1% of the time, Pallas kernels for 0%

commit v1 on v0

v1 whole, which is shorter than its diff:
```python
import jax
import jax.numpy as jnp
from jax import lax
from jax.experimental import pallas as pl
from jax.experimental.pallas import tpu as pltpu
from jax.sharding import PartitionSpec as P

MESH = pl.DeviceIdType.MESH
ZW = 8192.0
SEGS = 32
GYS = 16
F32 = jnp.float32


def hops(k):
    x, z = k // 8, k % 8
    return min(x, 4 - x) + min(z, 8 - z)


ORDER = sorted(
    ((k, h) for k in range(16) for h in (0, 1)), key=lambda kh: -hops((2 * kh[0] + kh[1]) % 32)
)


def roll_l(v, s):
    return pltpu.roll(v, s % 128, 1)


def roll_r(v, s):
    return pltpu.roll(v, s % 16, 0)


def swap_blocks(rows, blk):
    rows = list(rows)
    for bit in (1, 2, 4):
        keep = (blk & bit) == 0
        for i in range(8):
            if not i & bit:
                a, c = rows[i], rows[i | bit]
                rows[i] = jnp.where(keep, a, roll_l(c, 16 * bit))
                rows[i | bit] = jnp.where(keep, roll_l(a, -16 * bit), c)
    return rows


def face(a, b):
    total = a + b
    prod = a * b
    return jnp.where(prod > 0, 2.0 * prod / total, total)


def own_rows(half):
    return ((0, 4, 11), (5, 1, 11))[half]


def edge_rows(half):
    return ((13, 1, 3), (0, 12, 3))[half]


def eliminate(cond, excess, first_link, inv_ref, m_ref, h_ref, blk):
    zero = jnp.zeros_like(first_link)

    def step(i, carry):
        link_a, in_a, g_l, link_b, in_b, g_r = carry
        j = 30 - i
        g = excess[i] + in_a
        k = cond[i]
        inv = 1.0 / (link_a + k + g)
        m = k * inv
        h = link_a * inv
        inv_ref[i] = inv
        m_ref[i] = m
        h_ref[i] = h
        gb = excess[j] + in_b
        kb = cond[j - 1]
        invb = 1.0 / (link_b + kb + gb)
        mb = kb * invb
        hb = link_b * invb
        inv_ref[j] = invb
        m_ref[j] = mb
        h_ref[j] = hb
        return (link_a * m, g * m, g_l + g * h, link_b * mb, gb * mb, g_r + gb * hb)

    link_a, in_a, g_l, link_b, in_b, g_r = lax.fori_loop(
        0, 15, step, (first_link, zero, zero, cond[30], zero, zero), unroll=True
    )
    g = excess[15] + in_a + in_b
    inv = 1.0 / (link_a + link_b + g)
    ha = link_a * inv
    hb = link_b * inv
    inv_ref[15] = inv
    h_ref[15] = ha
    m_ref[15] = hb
    low = link_a * hb
    g_l = g_l + ha * g
    g_r = g_r + hb * g
    ground = excess[31] + g_r + roll_l(g_l, -16)
    up = roll_l(low, -16)
    factors = []
    for s in (16, 32, 64):
        inv = 1.0 / (low + up + ground)
        alpha = low * roll_l(inv, s)
        beta = up * roll_l(inv, -s)
        ground, low, up = (
            ground + alpha * roll_l(ground, s) + beta * roll_l(ground, -s),
            alpha * roll_l(low, s),
            beta * roll_l(up, -s),
        )
        factors.append((s, alpha, beta))
    return factors, 1.0 / ground


def line_solve(rhs, factors, inv_ref, m_ref, h_ref, b_ref, x_ref):
    seps, inv_sep = factors
    zero = jnp.zeros_like(inv_sep)

    def forward(i, carry):
        in_a, b_l, in_b, b_r = carry
        j = 30 - i
        b = rhs[i] + in_a
        bb = rhs[j] + in_b
        b_ref[i] = b
        b_ref[j] = bb
        return (m_ref[i] * b, b_l + h_ref[i] * b, m_ref[j] * bb, b_r + h_ref[j] * bb)

    in_a, b_l, in_b, b_r = lax.fori_loop(0, 15, forward, (zero, zero, zero, zero), unroll=True)
    mid = rhs[15] + in_a + in_b
    b_l = b_l + h_ref[15] * mid
    b_r = b_r + m_ref[15] * mid
    b = rhs[31] + b_r + roll_l(b_l, -16)
    for s, alpha, beta in seps:
        b = b + alpha * roll_l(b, s) + beta * roll_l(b, -s)
    x_r = b * inv_sep
    x_l = roll_l(x_r, 16)
    x_ref[31] = x_r
    mid = inv_ref[15] * mid + h_ref[15] * x_l + m_ref[15] * x_r
    x_ref[15] = mid

    def backward(n, carry):
        x_a, x_b = carry
        i = 14 - n
        j = 16 + n
        x_a = m_ref[i] * x_a + (inv_ref[i] * b_ref[i] + h_ref[i] * x_l)
        x_b = m_ref[j] * x_b + (inv_ref[j] * b_ref[j] + h_ref[j] * x_r)
        x_ref[i] = x_a
        x_ref[j] = x_b
        return (x_a, x_b)

    lax.fori_loop(0, 15, backward, (mid, mid), unroll=True)


def kernel(
    v_ref, imp_ref, mat_ref, o_ref,
    pack, recv, send_back, got_back, grid, cond, excess, rhs0, rhs1, fx, fy, ccond, cexcess,
    inv, m, h, cinv, cm, ch, bb, x0, x1, xc,
    send_sem, recv_sem, edge_send, edge_recv, back_send, back_recv,
):
    gy, gz = lax.axis_index("gy"), lax.axis_index("gz")
    half, tile = lax.rem(gz, 2), gz // 2
    above = lax.rem(gy + GYS - 1, GYS)
    below = lax.rem(gy + 1, GYS)
    mine_edge = lax.rem(gy + GYS - 1 + 2 * half, GYS)

    barrier = pltpu.get_barrier_semaphore()
    for k in sorted(range(SEGS), key=lambda k: -hops(k)):
        other = lax.rem(gz + k, SEGS)
        if k:
            pl.semaphore_signal(barrier, 1, device_id=(gy, other), device_id_type=MESH)
        pl.semaphore_signal(barrier, 1, device_id=(mine_edge, other), device_id_type=MESH)

    lane = lax.broadcasted_iota(jnp.int32, (16, 128), 1)
    row = lax.broadcasted_iota(jnp.int32, (16, 128), 0)
    blk = lane // 16
    win = lax.rem(lane, 16)

    for a in range(3):
        for odd in (0, 1):
            planes = []
            for z in range(8):
                v = v_ref[z]
                mat = mat_ref[z]
                if a == 0:
                    f = v
                elif a == 1:
                    f = jnp.where(mat == 0, 1.0, jnp.where(mat == 1, 0.33, 0.64)).astype(F32)
                else:
                    charge = 0.5 * imp_ref[z].astype(F32) - 1.5
                    f = jnp.where(mat == 0, jnp.exp(v) - jnp.exp(-v) - charge, 0.0)
                planes.append(roll_l(f, -4 if odd else 4))
            for t, f in enumerate(swap_blocks(planes, blk)):
                pack[2 * t + odd, a] = f

    pl.semaphore_wait(barrier, SEGS - 1 + SEGS)

    def own_copy(to, hf):
        s, d, n = own_rows(hf)
        return pltpu.make_async_remote_copy(
            src_ref=pack.at[to // 2, :, pl.ds(s, n)],
            dst_ref=recv.at[gz, :, pl.ds(d, n)],
            send_sem=send_sem.at[to],
            recv_sem=recv_sem.at[gz],
            device_id=(gy, to),
            device_id_type=MESH,
        )

    def edge_copy(to, hf):
        s, d, n = edge_rows(hf)
        return pltpu.make_async_remote_copy(
            src_ref=pack.at[to // 2, :, pl.ds(s, n)],
            dst_ref=recv.at[gz, :, pl.ds(d, n)],
            send_sem=edge_send.at[to],
            recv_sem=edge_recv.at[gz],
            device_id=(below if hf == 0 else above, to),
            device_id_type=MESH,
        )

    for k, hf in ORDER:
        to = 2 * lax.rem(tile + k, 16) + hf
        if k:
            own_copy(to, hf).start()
        else:

            @pl.when(half == hf)
            def _():
                s, d, n = own_rows(hf)
                pltpu.make_async_copy(
                    pack.at[to // 2, :, pl.ds(s, n)], recv.at[gz, :, pl.ds(d, n)], recv_sem.at[gz]
                ).start()

            @pl.when(half != hf)
            def _():
                own_copy(to, hf).start()

        edge_copy(to, hf).start()

    y = gy * 16 + half * 8 - 4 + row
    x = tile * 8 - 4 + win
    inside = (row >= 1) & (row <= 14) & (y >= 0) & (y < GYS * 16) & (x >= 0) & (x < 128)
    odd_cell = lax.rem(row + win, 2) == 1
    colour0 = inside & jnp.logical_not(odd_cell)
    colour1 = inside & odd_cell

    def landed(s):
        pltpu.make_async_copy(
            recv.at[0, :, pl.ds(1, 11)], recv.at[0, :, pl.ds(1, 11)], recv_sem.at[s]
        ).wait()
        pltpu.make_async_copy(
            recv.at[0, :, pl.ds(1, 3)], recv.at[0, :, pl.ds(1, 3)], edge_recv.at[s]
        ).wait()

    def take(q, carry):
        for c in range(8):
            landed(4 * c + q)
        for a in range(3):
            parts = swap_blocks([recv[4 * c + q, a] for c in range(8)], blk)
            for z in range(8):
                grid[a, 8 * q + z] = jnp.where(inside, parts[z], 0.0)
        return carry

    lax.fori_loop(0, 4, take, 0)

    for a in range(2):
        grid[a, 32] = jnp.where(blk == 7, 0.0, roll_l(grid[a, 0], -16))

    k_last = ZW * face(grid[1, 31], grid[1, 32])
    flow_last = k_last * (grid[0, 32] - grid[0, 31])
    k_floor = ZW * grid[1, 0]
    at_floor = blk == 0
    first_link = jnp.where(at_floor, 0.0, roll_l(k_last, 16))
    flow_first = jnp.where(at_floor, k_floor * grid[0, 0], roll_l(flow_last, 16))
    outside_one = jnp.where(inside, 0.0, 1.0)

    def assemble(i, flow_below):
        v = grid[0, i]
        p = grid[1, i]
        kz = ZW * face(p, grid[1, i + 1])
        flow = kz * (grid[0, i + 1] - v)
        px = face(p, roll_l(p, -1))
        py = face(p, roll_r(p, -1))
        flow_x = px * (roll_l(v, -1) - v)
        flow_y = py * (roll_r(v, -1) - v)
        soft = jnp.where(p == 1.0, jnp.exp(v) + jnp.exp(-v), 0.0) + outside_one
        extra = (px + roll_l(px, 1)) + (py + roll_r(py, 1)) + soft
        force = (
            (flow - flow_below) + (flow_x - roll_l(flow_x, 1)) + (flow_y - roll_r(flow_y, 1)) - grid[2, i]
        )
        cond[i] = kz
        excess[i] = extra
        fx[i] = px
        fy[i] = py
        rhs0[i] = jnp.where(colour0, force, 0.0)
        rhs1[i] = jnp.where(colour1, force, 0.0)
        k2 = kz + roll_l(kz, -1)
        ccond[i] = k2 + roll_r(k2, -1)
        e2 = extra + roll_l(extra, -1) - 2.0 * px
        y2 = py + roll_l(py, -1)
        cexcess[i] = e2 + roll_r(e2, -1) - 2.0 * y2
        return flow

    lax.fori_loop(0, 32, assemble, flow_first)

    def quad(f):
        f = f + roll_l(f, -1)
        return f + roll_r(f, -1)

    floor = jnp.where(at_floor, k_floor, 0.0)
    roof = jnp.where(blk == 7, k_last, 0.0)
    excess[0] = excess[0] + floor
    excess[31] = excess[31] + roof
    cexcess[0] = cexcess[0] + quad(floor)
    cexcess[31] = cexcess[31] + quad(roof)

    fine = eliminate(cond, excess, first_link, inv, m, h, blk)
    coarse = eliminate(ccond, cexcess, quad(first_link), cinv, cm, ch, blk)

    line_solve(rhs0, fine, inv, m, h, bb, x0)

    def lateral(f, i):
        gx, gyy = fx[i], fy[i]
        return (gx * roll_l(f, -1) + roll_l(gx * f, 1)) + (gyy * roll_r(f, -1) + roll_r(gyy * f, 1))

    def side(i, carry):
        rhs1[i] = jnp.where(colour1, rhs1[i] + lateral(x0[i], i), 0.0)
        return carry

    lax.fori_loop(0, 32, side, 0)
    line_solve(rhs1, fine, inv, m, h, bb, x1)

    def restrict(i, carry):
        rhs0[i] = quad(jnp.where(colour0, lateral(x1[i], i), 0.0))
        return carry

    lax.fori_loop(0, 32, restrict, 0)
    line_solve(rhs0, coarse, cinv, cm, ch, bb, xc)

    even_x = lax.rem(lane, 2) == 0
    even_y = lax.rem(row, 2) == 0

    def give(q, carry):
        parts = []
        for z in range(8):
            i = 8 * q + z
            f = xc[i]
            f = jnp.where(even_x, f, roll_l(f, 1))
            f = jnp.where(even_y, f, roll_r(f, 1))
            parts.append((x0[i] + x1[i] + f)[4:12])
        for c, f in enumerate(swap_blocks(parts, blk[:8])):
            send_back[4 * c + q] = f
        return carry

    lax.fori_loop(0, 4, give, 0)

    def back_copy(to):
        return pltpu.make_async_remote_copy(
            src_ref=send_back.at[to],
            dst_ref=got_back.at[gz],
            send_sem=back_send.at[to],
            recv_sem=back_recv.at[gz],
            device_id=(gy, to),
            device_id_type=MESH,
        )

    for k in sorted(range(SEGS), key=lambda k: -hops(k)):
        to = lax.rem(gz + k, SEGS)
        if k:
            back_copy(to).start()
    got_back[gz] = send_back[gz]

    for k, hf in ORDER:
        to = 2 * lax.rem(tile + k, 16) + hf
        if k:
            own_copy(to, hf).wait_send()
        else:

            @pl.when(half != hf)
            def _():
                own_copy(to, hf).wait_send()

        edge_copy(to, hf).wait_send()

    for k in range(1, SEGS):
        s = lax.rem(gz + k, SEGS)
        pltpu.make_async_copy(send_back.at[0], send_back.at[0], back_recv.at[s]).wait()

    low8 = win[:8] < 8
    for hf in (0, 1):
        parts = []
        for t in range(8):
            e = got_back[4 * t + hf]
            o = got_back[4 * t + 2 + hf]
            parts.append(jnp.where(low8, roll_l(e, -4), roll_l(o, 4)))
        for z, f in enumerate(swap_blocks(parts, blk[:8])):
            o_ref[z, pl.ds(8 * hf, 8)] = v_ref[z, pl.ds(8 * hf, 8)] + f

    for k in range(1, SEGS):
        s = lax.rem(gz + k, SEGS)
        pltpu.make_async_copy(send_back.at[0], send_back.at[0], back_send.at[s]).wait()


def body(electric_level, impurity_atoms, cell_materials):
    line = pltpu.VMEM((32, 16, 128), F32)
    vmem = pl.BlockSpec(memory_space=pltpu.VMEM)
    return pl.pallas_call(
        kernel,
        out_shape=jax.ShapeDtypeStruct(electric_level.shape, F32),
        in_specs=[vmem] * 3,
        out_specs=vmem,
        scratch_shapes=[
            pltpu.VMEM((16, 3, 16, 128), F32),
            pltpu.VMEM((SEGS, 3, 16, 128), F32),
            pltpu.VMEM((SEGS, 8, 128), F32),
            pltpu.VMEM((SEGS, 8, 128), F32),
            pltpu.VMEM((3, 33, 16, 128), F32),
        ]
        + [line] * 18
        + [pltpu.SemaphoreType.DMA((SEGS,))] * 6,
        compiler_params=pltpu.CompilerParams(
            collective_id=0, has_side_effects=True, vmem_limit_bytes=32 * 1024 * 1024
        ),
        cost_estimate=pl.CostEstimate(flops=20_000_000, bytes_accessed=262144, transcendentals=200_000),
        name="newton_step",
    )(electric_level, impurity_atoms, cell_materials)


def solution(mesh):
    placed = P("gz", "gy", None)
    return jax.shard_map(
        body, mesh=mesh, in_specs=(placed,) * 3, out_specs=placed, check_vma=False
    )
```

time: 1320 us -> 61.6 us (0.05)
  the two profiles are of different devices: /device:TPU:32 before, /device:TPU:1 now
where the time goes in v1:
time: 61.6 us; the launch traced here: 61.3 us
  Pallas kernels  58.1 us (94%)
  local copies, waits for them, and re-layouts  3.15 us (5%)
    pallas_call x1, Pallas kernels, body(): pl.pallas_call(kernel, out_shape=jax.ShapeDtypeStruct(electric_level.shap...  58.1 us
    unnamed x7, local copies, waits for them, and re-layouts  3.15 us

profile of v1, /device:TPU:1, one launch (start us, length us, event | category | flops | bytes accessed | tf_op | source)
XLA Modules:
  0.0 61.3 jit_solution(12813055988632852099)
XLA Ops:
  0.0 0.0 copy-start
  0.0 0.8 %copy-done = f32[8,16,128]{2,1,0:T(8,128)S(1)} copy-done((f32[8,16,128]{2,1,0:T(8,128)S(1)}, f32[8,16,128]{2,1,0:T(8,128)}, u32[]{:S(2)}) %copy-start) | copy-done | bytes 65560
  0.8 0.0 copy-start.1
  0.8 0.8 %copy-done.1 = s32[8,16,128]{2,1,0:T(8,128)S(1)} copy-done((s32[8,16,128]{2,1,0:T(8,128)S(1)}, s32[8,16,128]{2,1,0:T(8,128)}, u32[]{:S(2)}) %copy-start.1) | copy-done | bytes 65560
  1.7 0.0 copy-start.2
  1.7 0.8 %copy-done.2 = s32[8,16,128]{2,1,0:T(8,128)S(1)} copy-done((s32[8,16,128]{2,1,0:T(8,128)S(1)}, s32[8,16,128]{2,1,0:T(8,128)}, u32[]{:S(2)}) %copy-start.2) | copy-done | bytes 65560
  2.5 58.1 %newton_step.1 = f32[8,16,128]{2,1,0:T(8,128)S(1)} custom-call(f32[8,16,128]{2,1,0:T(8,128)S(1)} %copy-done, s32[8,16,128]{2,1,0:T(8,128)S(1)} %copy-done.1, s32[8,16,128]{2,1,0:T(8,128)S(1)} %copy-done.2), custom_call_target="tpu_custom_call" | custom-call | flops 20000000 | bytes 262144 | tf_op jit(solution)/shard_map/newton_step/pallas_call | solution.py:402
  60.7 0.6 %copy.5 = f32[8,16,128]{2,1,0:T(8,128)} copy(f32[8,16,128]{2,1,0:T(8,128)S(1)} %newton_step.1) | data formatting | bytes 131072
Async XLA Ops:
  0.0 0.8 %copy-start = (f32[8,16,128]{2,1,0:T(8,128)S(1)}, f32[8,16,128]{2,1,0:T(8,128)}, u32[]{:S(2)}) copy-start(f32[8,16,128]{2,1,0:T(8,128)} %v_ref.1) | copy-start | bytes 196612
  0.8 0.8 %copy-start.1 = (s32[8,16,128]{2,1,0:T(8,128)S(1)}, s32[8,16,128]{2,1,0:T(8,128)}, u32[]{:S(2)}) copy-start(s32[8,16,128]{2,1,0:T(8,128)} %imp_ref.1) | copy-start | bytes 196612
  1.7 0.8 %copy-start.2 = (s32[8,16,128]{2,1,0:T(8,128)S(1)}, s32[8,16,128]{2,1,0:T(8,128)}, u32[]{:S(2)}) copy-start(s32[8,16,128]{2,1,0:T(8,128)} %mat_ref.1) | copy-start | bytes 196612

commit v2 on v1

--- a/solution.py
+++ b/solution.py
@@ -149,8 +149,8 @@
 
 
 def kernel(
-    v_ref, imp_ref, mat_ref, o_ref,
-    pack, recv, send_back, got_back, grid, cond, excess, rhs0, rhs1, fx, fy, ccond, cexcess,
+    v_hbm, imp_hbm, mat_hbm, o_ref,
+    v_ref, imp_ref, mat_ref, in_sem, pack, recv, send_back, got_back, grid, cond, excess, rhs0, rhs1, fx, fy, ccond, cexcess,
     inv, m, h, cinv, cm, ch, bb, x0, x1, xc,
     send_sem, recv_sem, edge_send, edge_recv, back_send, back_recv,
 ):
@@ -160,6 +160,13 @@
     below = lax.rem(gy + 1, GYS)
     mine_edge = lax.rem(gy + GYS - 1 + 2 * half, GYS)
 
+    fetch = [
+        pltpu.make_async_copy(v_hbm, v_ref, in_sem.at[0]),
+        pltpu.make_async_copy(mat_hbm, mat_ref, in_sem.at[1]),
+        pltpu.make_async_copy(imp_hbm, imp_ref, in_sem.at[2]),
+    ]
+    for copy in fetch:
+        copy.start()
     barrier = pltpu.get_barrier_semaphore()
     for k in sorted(range(SEGS), key=lambda k: -hops(k)):
         other = lax.rem(gz + k, SEGS)
@@ -171,6 +178,9 @@
     row = lax.broadcasted_iota(jnp.int32, (16, 128), 0)
     blk = lane // 16
     win = lax.rem(lane, 16)
+
+    for copy in fetch:
+        copy.wait()
 
     for a in range(3):
         for odd in (0, 1):
@@ -256,7 +266,7 @@
                 grid[a, 8 * q + z] = jnp.where(inside, parts[z], 0.0)
         return carry
 
-    lax.fori_loop(0, 4, take, 0)
+    lax.fori_loop(0, 4, take, 0, unroll=4)
 
     for a in range(2):
         grid[a, 32] = jnp.where(blk == 7, 0.0, roll_l(grid[a, 0], -16))
@@ -296,7 +306,7 @@
         cexcess[i] = e2 + roll_r(e2, -1) - 2.0 * y2
         return flow
 
-    lax.fori_loop(0, 32, assemble, flow_first)
+    lax.fori_loop(0, 32, assemble, flow_first, unroll=32)
 
     def quad(f):
         f = f + roll_l(f, -1)
@@ -322,14 +332,14 @@
         rhs1[i] = jnp.where(colour1, rhs1[i] + lateral(x0[i], i), 0.0)
         return carry
 
-    lax.fori_loop(0, 32, side, 0)
+    lax.fori_loop(0, 32, side, 0, unroll=32)
     line_solve(rhs1, fine, inv, m, h, bb, x1)
 
     def restrict(i, carry):
         rhs0[i] = quad(jnp.where(colour0, lateral(x1[i], i), 0.0))
         return carry
 
-    lax.fori_loop(0, 32, restrict, 0)
+    lax.fori_loop(0, 32, restrict, 0, unroll=32)
     line_solve(rhs0, coarse, cinv, cm, ch, bb, xc)
 
     even_x = lax.rem(lane, 2) == 0
@@ -347,7 +357,7 @@
             send_back[4 * c + q] = f
         return carry
 
-    lax.fori_loop(0, 4, give, 0)
+    lax.fori_loop(0, 4, give, 0, unroll=4)
 
     def back_copy(to):
         return pltpu.make_async_remote_copy(
@@ -402,9 +412,13 @@
     return pl.pallas_call(
         kernel,
         out_shape=jax.ShapeDtypeStruct(electric_level.shape, F32),
-        in_specs=[vmem] * 3,
+        in_specs=[pl.BlockSpec(memory_space=pltpu.HBM)] * 3,
         out_specs=vmem,
         scratch_shapes=[
+            pltpu.VMEM(electric_level.shape, F32),
+            pltpu.VMEM(electric_level.shape, jnp.int32),
+            pltpu.VMEM(electric_level.shape, jnp.int32),
+            pltpu.SemaphoreType.DMA((3,)),
             pltpu.VMEM((16, 3, 16, 128), F32),
             pltpu.VMEM((SEGS, 3, 16, 128), F32),
             pltpu.VMEM((SEGS, 8, 128), F32),

time: 61.6 us -> 47.1 us (0.76)
  Pallas kernels: 58.1 us -> 43.7 us
    pallas_call x1, Pallas kernels: 58.1 us -> 43.7 us  [body(): pl.pallas_call(kernel, out_shape=jax.ShapeDtypeStruct(electric_level.shap...]
where the time goes in v2:
time: 47.1 us; the launch traced here: 46.9 us
  Pallas kernels  43.7 us (93%)
  local copies, waits for them, and re-layouts  3.15 us (7%)
    pallas_call x1, Pallas kernels, body(): pl.pallas_call(kernel, out_shape=jax.ShapeDtypeStruct(electric_level.shap...  43.7 us
    unnamed x7, local copies, waits for them, and re-layouts  3.15 us

profile of v2, /device:TPU:1, one launch (start us, length us, event | category | flops | bytes accessed | tf_op | source)
XLA Modules:
  0.0 46.9 jit_solution(11738074846350052216)
XLA Ops:
  0.0 0.0 copy-start
  0.0 0.8 %copy-done = f32[8,16,128]{2,1,0:T(8,128)S(1)} copy-done((f32[8,16,128]{2,1,0:T(8,128)S(1)}, f32[8,16,128]{2,1,0:T(8,128)}, u32[]{:S(2)}) %copy-start) | copy-done | bytes 65560
  0.8 0.0 copy-start.1
  0.8 0.8 %copy-done.1 = s32[8,16,128]{2,1,0:T(8,128)S(1)} copy-done((s32[8,16,128]{2,1,0:T(8,128)S(1)}, s32[8,16,128]{2,1,0:T(8,128)}, u32[]{:S(2)}) %copy-start.1) | copy-done | bytes 65560
  1.7 0.0 copy-start.2
  1.7 0.8 %copy-done.2 = s32[8,16,128]{2,1,0:T(8,128)S(1)} copy-done((s32[8,16,128]{2,1,0:T(8,128)S(1)}, s32[8,16,128]{2,1,0:T(8,128)}, u32[]{:S(2)}) %copy-start.2) | copy-done | bytes 65560
  2.5 43.7 %newton_step.1 = f32[8,16,128]{2,1,0:T(8,128)S(1)} custom-call(f32[8,16,128]{2,1,0:T(8,128)S(1)} %copy-done, s32[8,16,128]{2,1,0:T(8,128)S(1)} %copy-done.1, s32[8,16,128]{2,1,0:T(8,128)S(1)} %copy-done.2), custom_call_target="tpu_custom_call" | custom-call | flops 20000000 | bytes 262144 | tf_op jit(solution)/shard_map/newton_step/pallas_call | solution.py:412
  46.2 0.6 %copy.5 = f32[8,16,128]{2,1,0:T(8,128)} copy(f32[8,16,128]{2,1,0:T(8,128)S(1)} %newton_step.1) | data formatting | bytes 131072
Async XLA Ops:
  0.0 0.8 %copy-start = (f32[8,16,128]{2,1,0:T(8,128)S(1)}, f32[8,16,128]{2,1,0:T(8,128)}, u32[]{:S(2)}) copy-start(f32[8,16,128]{2,1,0:T(8,128)} %v_hbm.1) | copy-start | bytes 196612
  0.8 0.8 %copy-start.1 = (s32[8,16,128]{2,1,0:T(8,128)S(1)}, s32[8,16,128]{2,1,0:T(8,128)}, u32[]{:S(2)}) copy-start(s32[8,16,128]{2,1,0:T(8,128)} %imp_hbm.1) | copy-start | bytes 196612
  1.7 0.8 %copy-start.2 = (s32[8,16,128]{2,1,0:T(8,128)S(1)}, s32[8,16,128]{2,1,0:T(8,128)}, u32[]{:S(2)}) copy-start(s32[8,16,128]{2,1,0:T(8,128)} %mat_hbm.1) | copy-start | bytes 196612

commit v3 on v2

--- a/solution.py
+++ b/solution.py
@@ -17,9 +17,8 @@
     return min(x, 4 - x) + min(z, 8 - z)
 
 
-ORDER = sorted(
-    ((k, h) for k in range(16) for h in (0, 1)), key=lambda kh: -hops((2 * kh[0] + kh[1]) % 32)
-)
+FAR_FIRST = sorted(range(SEGS), key=lambda k: -hops(k))
+TILES_FAR_FIRST = sorted(range(16), key=lambda k: -hops(2 * k))
 
 
 def roll_l(v, s):
@@ -48,12 +47,11 @@
     return jnp.where(prod > 0, 2.0 * prod / total, total)
 
 
-def own_rows(half):
-    return ((0, 4, 11), (5, 1, 11))[half]
-
-
-def edge_rows(half):
-    return ((13, 1, 3), (0, 12, 3))[half]
+MAIN = ((0, 4, 8), (8, 4, 8))
+LOWER = (13, 1, 3)
+UPPER = (0, 12, 3)
+FORWARD = ((9, 1, 3), (4, 12, 3))
+FIELDS = ((0, 2), (2, 1))
 
 
 def eliminate(cond, excess, first_link, inv_ref, m_ref, h_ref, blk):
@@ -150,15 +148,15 @@
 
 def kernel(
     v_hbm, imp_hbm, mat_hbm, o_ref,
-    v_ref, imp_ref, mat_ref, in_sem, pack, recv, send_back, got_back, grid, cond, excess, rhs0, rhs1, fx, fy, ccond, cexcess,
-    inv, m, h, cinv, cm, ch, bb, x0, x1, xc,
-    send_sem, recv_sem, edge_send, edge_recv, back_send, back_recv,
+    v_ref, imp_ref, mat_ref, in_sem, pack, recv, send_back, got_back, grid,
+    cond, excess, rhs0, rhs1, fx, fy, ccond, cexcess, inv, m, h, cinv, cm, ch, bb, x0, x1, xc,
+    main_send, edge_send, main_recv, edge_recv, fwd_send, fwd_recv, back_send, back_recv,
 ):
     gy, gz = lax.axis_index("gy"), lax.axis_index("gz")
-    half, tile = lax.rem(gz, 2), gz // 2
-    above = lax.rem(gy + GYS - 1, GYS)
-    below = lax.rem(gy + 1, GYS)
-    mine_edge = lax.rem(gy + GYS - 1 + 2 * half, GYS)
+    core, par, tile = lax.rem(gy, 2), lax.rem(gz, 2), gz // 2
+    chip = gy - core
+    strip = chip + par
+    edge_from = lax.rem(strip + GYS - 1 + 2 * core, GYS)
 
     fetch = [
         pltpu.make_async_copy(v_hbm, v_ref, in_sem.at[0]),
@@ -167,12 +165,27 @@
     ]
     for copy in fetch:
         copy.start()
+
+    def hello(*device):
+        pl.semaphore_signal(barrier, 1, device_id=device, device_id_type=MESH)
+
     barrier = pltpu.get_barrier_semaphore()
-    for k in sorted(range(SEGS), key=lambda k: -hops(k)):
+    for k in FAR_FIRST:
         other = lax.rem(gz + k, SEGS)
         if k:
-            pl.semaphore_signal(barrier, 1, device_id=(gy, other), device_id_type=MESH)
-        pl.semaphore_signal(barrier, 1, device_id=(mine_edge, other), device_id_type=MESH)
+            hello(strip, other)
+            hello(edge_from, other)
+        else:
+
+            @pl.when(strip != gy)
+            def _():
+                hello(strip, other)
+
+            @pl.when(edge_from != gy)
+            def _():
+                hello(edge_from, other)
+
+            hello(chip + 1 - core, gz)
 
     lane = lax.broadcasted_iota(jnp.int32, (16, 128), 1)
     row = lax.broadcasted_iota(jnp.int32, (16, 128), 0)
@@ -199,74 +212,116 @@
             for t, f in enumerate(swap_blocks(planes, blk)):
                 pack[2 * t + odd, a] = f
 
-    pl.semaphore_wait(barrier, SEGS - 1 + SEGS)
-
-    def own_copy(to, hf):
-        s, d, n = own_rows(hf)
+    pl.semaphore_wait(barrier, 2 * SEGS)
+
+    def copy_of(part, j, rows, device, send, got):
+        a, n = FIELDS[part]
+        src, dst, count = rows
         return pltpu.make_async_remote_copy(
-            src_ref=pack.at[to // 2, :, pl.ds(s, n)],
-            dst_ref=recv.at[gz, :, pl.ds(d, n)],
-            send_sem=send_sem.at[to],
-            recv_sem=recv_sem.at[gz],
-            device_id=(gy, to),
+            src_ref=pack.at[j, pl.ds(a, n), pl.ds(src, count)],
+            dst_ref=recv.at[gz // 4, lax.rem(gz, 4), pl.ds(a, n), pl.ds(dst, count)],
+            send_sem=send,
+            recv_sem=got,
+            device_id=device,
             device_id_type=MESH,
         )
 
-    def edge_copy(to, hf):
-        s, d, n = edge_rows(hf)
-        return pltpu.make_async_remote_copy(
-            src_ref=pack.at[to // 2, :, pl.ds(s, n)],
-            dst_ref=recv.at[gz, :, pl.ds(d, n)],
-            send_sem=edge_send.at[to],
-            recv_sem=edge_recv.at[gz],
-            device_id=(below if hf == 0 else above, to),
-            device_id_type=MESH,
+    def main_copy(part, k, to_core):
+        j = lax.rem(tile + k, 16)
+        return copy_of(
+            part, j, MAIN[to_core], (chip + to_core, 2 * j + core),
+            main_send.at[part, to_core, k], main_recv.at[part, gz],
         )
 
-    for k, hf in ORDER:
-        to = 2 * lax.rem(tile + k, 16) + hf
-        if k:
-            own_copy(to, hf).start()
-        else:
-
-            @pl.when(half == hf)
-            def _():
-                s, d, n = own_rows(hf)
-                pltpu.make_async_copy(
-                    pack.at[to // 2, :, pl.ds(s, n)], recv.at[gz, :, pl.ds(d, n)], recv_sem.at[gz]
-                ).start()
-
-            @pl.when(half != hf)
-            def _():
-                own_copy(to, hf).start()
-
-        edge_copy(to, hf).start()
-
-    y = gy * 16 + half * 8 - 4 + row
+    def edge_copy(part, k, upper):
+        j = lax.rem(tile + k, 16)
+        to = lax.rem(gy + core + (GYS - 1 if upper else 0), GYS)
+        return copy_of(
+            part, j, UPPER if upper else LOWER, (to, 2 * j + 1 - core),
+            edge_send.at[part, upper, k], edge_recv.at[part, gz],
+        )
+
+    def keep(part, rows, got):
+        a, n = FIELDS[part]
+        src, dst, count = rows
+        pltpu.make_async_copy(
+            pack.at[tile, pl.ds(a, n), pl.ds(src, count)],
+            recv.at[gz // 4, lax.rem(gz, 4), pl.ds(a, n), pl.ds(dst, count)],
+            got.at[part, gz],
+        ).start()
+
+    main_self = [(par == core) & (core == to_core) for to_core in (0, 1)]
+    edge_self = [(core == 0) & (par == 1), (core == 1) & (par == 0)]
+
+    for part in (0, 1):
+        for k in TILES_FAR_FIRST:
+            for w in (0, 1):
+                if k:
+                    main_copy(part, k, w).start()
+                    edge_copy(part, k, w).start()
+                else:
+
+                    @pl.when(main_self[w])
+                    def _():
+                        keep(part, MAIN[w], main_recv)
+
+                    @pl.when(jnp.logical_not(main_self[w]))
+                    def _():
+                        main_copy(part, k, w).start()
+
+                    @pl.when(edge_self[w])
+                    def _():
+                        keep(part, UPPER if w else LOWER, edge_recv)
+
+                    @pl.when(jnp.logical_not(edge_self[w]))
+                    def _():
+                        edge_copy(part, k, w).start()
+
+    y = strip * 16 + core * 8 - 4 + row
     x = tile * 8 - 4 + win
     inside = (row >= 1) & (row <= 14) & (y >= 0) & (y < GYS * 16) & (x >= 0) & (x < 128)
     odd_cell = lax.rem(row + win, 2) == 1
     colour0 = inside & jnp.logical_not(odd_cell)
     colour1 = inside & odd_cell
 
-    def landed(s):
-        pltpu.make_async_copy(
-            recv.at[0, :, pl.ds(1, 11)], recv.at[0, :, pl.ds(1, 11)], recv_sem.at[s]
-        ).wait()
-        pltpu.make_async_copy(
-            recv.at[0, :, pl.ds(1, 3)], recv.at[0, :, pl.ds(1, 3)], edge_recv.at[s]
-        ).wait()
-
-    def take(q, carry):
-        for c in range(8):
-            landed(4 * c + q)
-        for a in range(3):
-            parts = swap_blocks([recv[4 * c + q, a] for c in range(8)], blk)
+    def forward_copy(part, q, frm):
+        a, n = FIELDS[part]
+        src, dst, count = FORWARD[frm]
+        return pltpu.make_async_remote_copy(
+            src_ref=recv.at[:, q, pl.ds(a, n), pl.ds(src, count)],
+            dst_ref=recv.at[:, q, pl.ds(a, n), pl.ds(dst, count)],
+            send_sem=fwd_send.at[part, q],
+            recv_sem=fwd_recv.at[part, q],
+            device_id=(chip + 1 - frm, gz),
+            device_id_type=MESH,
+        )
+
+    def forward(part):
+        a, n = FIELDS[part]
+        for q in range(4):
+            for c in range(8):
+                s = 4 * c + q
+                for count, sem in ((8, main_recv), (3, edge_recv)):
+                    piece = recv.at[0, 0, pl.ds(a, n), pl.ds(4, count)]
+                    pltpu.make_async_copy(piece, piece, sem.at[part, s]).wait()
+            for frm in (0, 1):
+
+                @pl.when(core == frm)
+                def _():
+                    forward_copy(part, q, frm).start()
+
+    def forwarded(part, q):
+        a, n = FIELDS[part]
+        piece = recv.at[:, 0, pl.ds(a, n), pl.ds(4, 3)]
+        pltpu.make_async_copy(piece, piece, fwd_recv.at[part, q]).wait()
+
+    forward(0)
+    for q in range(4):
+        forwarded(0, q)
+        for a in range(2):
+            parts = swap_blocks([recv[c, q, a] for c in range(8)], blk)
             for z in range(8):
                 grid[a, 8 * q + z] = jnp.where(inside, parts[z], 0.0)
-        return carry
-
-    lax.fori_loop(0, 4, take, 0, unroll=4)
 
     for a in range(2):
         grid[a, 32] = jnp.where(blk == 7, 0.0, roll_l(grid[a, 0], -16))
@@ -290,15 +345,11 @@
         flow_y = py * (roll_r(v, -1) - v)
         soft = jnp.where(p == 1.0, jnp.exp(v) + jnp.exp(-v), 0.0) + outside_one
         extra = (px + roll_l(px, 1)) + (py + roll_r(py, 1)) + soft
-        force = (
-            (flow - flow_below) + (flow_x - roll_l(flow_x, 1)) + (flow_y - roll_r(flow_y, 1)) - grid[2, i]
-        )
+        rhs0[i] = (flow - flow_below) + (flow_x - roll_l(flow_x, 1)) + (flow_y - roll_r(flow_y, 1))
         cond[i] = kz
         excess[i] = extra
         fx[i] = px
         fy[i] = py
-        rhs0[i] = jnp.where(colour0, force, 0.0)
-        rhs1[i] = jnp.where(colour1, force, 0.0)
         k2 = kz + roll_l(kz, -1)
         ccond[i] = k2 + roll_r(k2, -1)
         e2 = extra + roll_l(extra, -1) - 2.0 * px
@@ -322,6 +373,15 @@
     fine = eliminate(cond, excess, first_link, inv, m, h, blk)
     coarse = eliminate(ccond, cexcess, quad(first_link), cinv, cm, ch, blk)
 
+    forward(1)
+    for q in range(4):
+        forwarded(1, q)
+        parts = swap_blocks([recv[c, q, 2] for c in range(8)], blk)
+        for z in range(8):
+            force = rhs0[8 * q + z] - parts[z]
+            rhs0[8 * q + z] = jnp.where(colour0, force, 0.0)
+            rhs1[8 * q + z] = jnp.where(colour1, force, 0.0)
+
     line_solve(rhs0, fine, inv, m, h, bb, x0)
 
     def lateral(f, i):
@@ -345,7 +405,7 @@
     even_x = lax.rem(lane, 2) == 0
     even_y = lax.rem(row, 2) == 0
 
-    def give(q, carry):
+    for q in range(4):
         parts = []
         for z in range(8):
             i = 8 * q + z
@@ -355,58 +415,84 @@
             parts.append((x0[i] + x1[i] + f)[4:12])
         for c, f in enumerate(swap_blocks(parts, blk[:8])):
             send_back[4 * c + q] = f
-        return carry
-
-    lax.fori_loop(0, 4, give, 0, unroll=4)
+
+    slot = core * 16 + tile
 
     def back_copy(to):
         return pltpu.make_async_remote_copy(
             src_ref=send_back.at[to],
-            dst_ref=got_back.at[gz],
+            dst_ref=got_back.at[slot],
             send_sem=back_send.at[to],
-            recv_sem=back_recv.at[gz],
-            device_id=(gy, to),
+            recv_sem=back_recv.at[slot],
+            device_id=(strip, to),
             device_id_type=MESH,
         )
 
-    for k in sorted(range(SEGS), key=lambda k: -hops(k)):
+    for k in FAR_FIRST:
         to = lax.rem(gz + k, SEGS)
         if k:
             back_copy(to).start()
-    got_back[gz] = send_back[gz]
-
-    for k, hf in ORDER:
-        to = 2 * lax.rem(tile + k, 16) + hf
-        if k:
-            own_copy(to, hf).wait_send()
         else:
 
-            @pl.when(half != hf)
+            @pl.when(strip == gy)
             def _():
-                own_copy(to, hf).wait_send()
-
-        edge_copy(to, hf).wait_send()
-
-    for k in range(1, SEGS):
-        s = lax.rem(gz + k, SEGS)
-        pltpu.make_async_copy(send_back.at[0], send_back.at[0], back_recv.at[s]).wait()
+                pltpu.make_async_copy(
+                    send_back.at[gz], got_back.at[slot], back_recv.at[slot]
+                ).start()
+
+            @pl.when(strip != gy)
+            def _():
+                back_copy(to).start()
+
+    for part in (0, 1):
+        for k in range(16):
+            for w in (0, 1):
+                if k:
+                    main_copy(part, k, w).wait_send()
+                    edge_copy(part, k, w).wait_send()
+                else:
+
+                    @pl.when(jnp.logical_not(main_self[w]))
+                    def _():
+                        main_copy(part, k, w).wait_send()
+
+                    @pl.when(jnp.logical_not(edge_self[w]))
+                    def _():
+                        edge_copy(part, k, w).wait_send()
+
+        for q in range(4):
+            for frm in (0, 1):
+
+                @pl.when(core == frm)
+                def _():
+                    forward_copy(part, q, frm).wait_send()
+
+    for k in range(SEGS):
+        pltpu.make_async_copy(send_back.at[0], send_back.at[0], back_recv.at[k]).wait()
 
     low8 = win[:8] < 8
-    for hf in (0, 1):
+    for to_core in (0, 1):
         parts = []
         for t in range(8):
-            e = got_back[4 * t + hf]
-            o = got_back[4 * t + 2 + hf]
+            e = got_back[16 * to_core + 2 * t]
+            o = got_back[16 * to_core + 2 * t + 1]
             parts.append(jnp.where(low8, roll_l(e, -4), roll_l(o, 4)))
         for z, f in enumerate(swap_blocks(parts, blk[:8])):
-            o_ref[z, pl.ds(8 * hf, 8)] = v_ref[z, pl.ds(8 * hf, 8)] + f
-
-    for k in range(1, SEGS):
-        s = lax.rem(gz + k, SEGS)
-        pltpu.make_async_copy(send_back.at[0], send_back.at[0], back_send.at[s]).wait()
+            o_ref[z, pl.ds(8 * to_core, 8)] = v_ref[z, pl.ds(8 * to_core, 8)] + f
+
+    for k in range(SEGS):
+        if k:
+            to = lax.rem(gz + k, SEGS)
+            back_copy(to).wait_send()
+        else:
+
+            @pl.when(strip != gy)
+            def _():
+                back_copy(gz).wait_send()
 
 
 def body(electric_level, impurity_atoms, cell_materials):
+    fields = (electric_level, impurity_atoms, cell_materials)
     line = pltpu.VMEM((32, 16, 128), F32)
     vmem = pl.BlockSpec(memory_space=pltpu.VMEM)
     return pl.pallas_call(
@@ -420,19 +506,22 @@
             pltpu.VMEM(electric_level.shape, jnp.int32),
             pltpu.SemaphoreType.DMA((3,)),
             pltpu.VMEM((16, 3, 16, 128), F32),
-            pltpu.VMEM((SEGS, 3, 16, 128), F32),
+            pltpu.VMEM((8, 4, 3, 16, 128), F32),
             pltpu.VMEM((SEGS, 8, 128), F32),
             pltpu.VMEM((SEGS, 8, 128), F32),
-            pltpu.VMEM((3, 33, 16, 128), F32),
+            pltpu.VMEM((2, 33, 16, 128), F32),
         ]
         + [line] * 18
-        + [pltpu.SemaphoreType.DMA((SEGS,))] * 6,
+        + [pltpu.SemaphoreType.DMA((2, 2, 16))] * 2
+        + [pltpu.SemaphoreType.DMA((2, SEGS))] * 2
+        + [pltpu.SemaphoreType.DMA((2, 4))] * 2
+        + [pltpu.SemaphoreType.DMA((SEGS,))] * 2,
         compiler_params=pltpu.CompilerParams(
             collective_id=0, has_side_effects=True, vmem_limit_bytes=32 * 1024 * 1024
         ),
         cost_estimate=pl.CostEstimate(flops=20_000_000, bytes_accessed=262144, transcendentals=200_000),
         name="newton_step",
-    )(electric_level, impurity_atoms, cell_materials)
+    )(*(pltpu.with_memory_space_constraint(f, pltpu.HBM) for f in fields))
 
 
 def solution(mesh):

time: 47.1 us -> 46 us (0.977)
  local copies, waits for them, and re-layouts: 3.15 us -> 0.63 us
  Pallas kernels: 43.7 us -> 45.2 us
    unnamed x7 -> x1, local copies, waits for them, and re-layouts: 3.15 us -> 0.63 us
    pallas_call x1, Pallas kernels: 43.7 us -> 45.2 us  [body(): pl.pallas_call(kernel, out_shape=jax.ShapeDtypeStruct(electric_level.shap...]
where the time goes in v3:
time: 46 us; the launch traced here: 45.8 us
  Pallas kernels  45.2 us (98%)
  local copies, waits for them, and re-layouts  0.63 us (1%)
    pallas_call x1, Pallas kernels, body(): pl.pallas_call(kernel, out_shape=jax.ShapeDtypeStruct(electric_level.shap...  45.2 us

profile of v3, /device:TPU:1, one launch (start us, length us, event | category | flops | bytes accessed | tf_op | source)
XLA Modules:
  0.0 45.8 jit_solution(13794557517071346370)
XLA Ops:
  0.0 45.2 %newton_step.1 = f32[8,16,128]{2,1,0:T(8,128)S(1)} custom-call(f32[8,16,128]{2,1,0:T(8,128)} %v_hbm.1, s32[8,16,128]{2,1,0:T(8,128)} %imp_hbm.1, s32[8,16,128]{2,1,0:T(8,128)} %mat_hbm.1), custom_call_target="tpu_custom_call" | custom-call | flops 20000000 | bytes 262144 | tf_op jit(solution)/shard_map/newton_step/pallas_call | solution.py:498
  45.2 0.6 %copy.5 = f32[8,16,128]{2,1,0:T(8,128)} copy(f32[8,16,128]{2,1,0:T(8,128)S(1)} %newton_step.1) | data formatting | bytes 131072

commit v4 on v3

v4 whole, which is shorter than its diff:
```python
import jax
import jax.numpy as jnp
from jax import lax
from jax.experimental import pallas as pl
from jax.experimental.pallas import tpu as pltpu
from jax.sharding import PartitionSpec as P

MESH = pl.DeviceIdType.MESH
ZW = 8192.0
SEGS = 32
GYS = 16
F32 = jnp.float32


def hops(k):
    x, z = k // 8, k % 8
    return min(x, 4 - x) + min(z, 8 - z)


FAR_FIRST = sorted(range(SEGS), key=lambda k: -hops(k))
WIDE = 10
TILES = 13
OWNERS = 2 * TILES
TILES_FAR_FIRST = sorted(range(TILES), key=lambda k: -hops((SEGS * k // TILES) % SEGS))


def owner_place(n):
    return (16 * n) // TILES


def roll_l(v, s):
    return pltpu.roll(v, s % 128, 1)


def roll_r(v, s):
    return pltpu.roll(v, s % 16, 0)


def swap_blocks(rows, blk):
    rows = list(rows)
    for bit in (1, 2, 4):
        keep = (blk & bit) == 0
        for i in range(8):
            if not i & bit:
                a, c = rows[i], rows[i | bit]
                rows[i] = jnp.where(keep, a, roll_l(c, 16 * bit))
                rows[i | bit] = jnp.where(keep, roll_l(a, -16 * bit), c)
    return rows


def face(a, b):
    total = a + b
    prod = a * b
    return jnp.where(prod > 0, 2.0 * prod / total, total)


MAIN = ((0, 4, 8), (8, 4, 8))
LOWER = ((13, 1, 3), (14, 2, 2))
UPPER = ((0, 12, 3), (0, 12, 2))
FORWARD = (((9, 1, 3), (4, 12, 3)), ((10, 2, 2), (4, 12, 2)))
FIELDS = ((0, 2), (2, 1))


def eliminate(cond, excess, first_link, inv_ref, m_ref, h_ref, blk):
    zero = jnp.zeros_like(first_link)

    def step(i, carry):
        link_a, in_a, g_l, link_b, in_b, g_r = carry
        j = 30 - i
        g = excess[i] + in_a
        k = cond[i]
        inv = 1.0 / (link_a + k + g)
        m = k * inv
        h = link_a * inv
        inv_ref[i] = inv
        m_ref[i] = m
        h_ref[i] = h
        gb = excess[j] + in_b
        kb = cond[j - 1]
        invb = 1.0 / (link_b + kb + gb)
        mb = kb * invb
        hb = link_b * invb
        inv_ref[j] = invb
        m_ref[j] = mb
        h_ref[j] = hb
        return (link_a * m, g * m, g_l + g * h, link_b * mb, gb * mb, g_r + gb * hb)

    link_a, in_a, g_l, link_b, in_b, g_r = lax.fori_loop(
        0, 15, step, (first_link, zero, zero, cond[30], zero, zero), unroll=True
    )
    g = excess[15] + in_a + in_b
    inv = 1.0 / (link_a + link_b + g)
    ha = link_a * inv
    hb = link_b * inv
    inv_ref[15] = inv
    h_ref[15] = ha
    m_ref[15] = hb
    low = link_a * hb
    g_l = g_l + ha * g
    g_r = g_r + hb * g
    ground = excess[31] + g_r + roll_l(g_l, -16)
    up = roll_l(low, -16)
    factors = []
    for s in (16, 32, 64):
        inv = 1.0 / (low + up + ground)
        alpha = low * roll_l(inv, s)
        beta = up * roll_l(inv, -s)
        ground, low, up = (
            ground + alpha * roll_l(ground, s) + beta * roll_l(ground, -s),
            alpha * roll_l(low, s),
            beta * roll_l(up, -s),
        )
        factors.append((s, alpha, beta))
    return factors, 1.0 / ground


def line_solve(rhs, factors, inv_ref, m_ref, h_ref, b_ref, x_ref):
    seps, inv_sep = factors
    zero = jnp.zeros_like(inv_sep)

    def forward(i, carry):
        in_a, b_l, in_b, b_r = carry
        j = 30 - i
        b = rhs[i] + in_a
        bb = rhs[j] + in_b
        b_ref[i] = b
        b_ref[j] = bb
        return (m_ref[i] * b, b_l + h_ref[i] * b, m_ref[j] * bb, b_r + h_ref[j] * bb)

    in_a, b_l, in_b, b_r = lax.fori_loop(0, 15, forward, (zero, zero, zero, zero), unroll=True)
    mid = rhs[15] + in_a + in_b
    b_l = b_l + h_ref[15] * mid
    b_r = b_r + m_ref[15] * mid
    b = rhs[31] + b_r + roll_l(b_l, -16)
    for s, alpha, beta in seps:
        b = b + alpha * roll_l(b, s) + beta * roll_l(b, -s)
    x_r = b * inv_sep
    x_l = roll_l(x_r, 16)
    x_ref[31] = x_r
    mid = inv_ref[15] * mid + h_ref[15] * x_l + m_ref[15] * x_r
    x_ref[15] = mid

    def backward(n, carry):
        x_a, x_b = carry
        i = 14 - n
        j = 16 + n
        x_a = m_ref[i] * x_a + (inv_ref[i] * b_ref[i] + h_ref[i] * x_l)
        x_b = m_ref[j] * x_b + (inv_ref[j] * b_ref[j] + h_ref[j] * x_r)
        x_ref[i] = x_a
        x_ref[j] = x_b
        return (x_a, x_b)

    lax.fori_loop(0, 15, backward, (mid, mid), unroll=True)


def kernel(
    v_hbm, imp_hbm, mat_hbm, o_ref,
    v_ref, imp_ref, mat_ref, in_sem, pack, recv, send_back, got_back, grid,
    cond, excess, rhs0, rhs1, fx, fy, ccond, cexcess, inv, m, h, cinv, cm, ch, bb, x0, x1, xc,
    main_send, edge_send, main_recv, edge_recv, fwd_send, fwd_recv, back_send, back_recv,
):
    gy, gz = lax.axis_index("gy"), lax.axis_index("gz")
    core = lax.rem(gy, 2)
    number = (TILES * gz + 15) // 16
    owner = (number < OWNERS) & (owner_place(number) == gz)
    par, tile = lax.rem(number, 2), lax.rem(number // 2, TILES)
    chip = gy - core
    strip = chip + par
    edge_from = lax.rem(strip + GYS - 1 + 2 * core, GYS)

    fetch = [
        pltpu.make_async_copy(v_hbm, v_ref, in_sem.at[0]),
        pltpu.make_async_copy(mat_hbm, mat_ref, in_sem.at[1]),
        pltpu.make_async_copy(imp_hbm, imp_ref, in_sem.at[2]),
    ]
    for copy in fetch:
        copy.start()

    def hello(*device):
        pl.semaphore_signal(barrier, 1, device_id=device, device_id_type=MESH)

    barrier = pltpu.get_barrier_semaphore()

    @pl.when(owner)
    def _():
        for k in FAR_FIRST:
            other = lax.rem(gz + k, SEGS)
            if k:
                hello(strip, other)
                hello(edge_from, other)
            else:

                @pl.when(strip != gy)
                def _():
                    hello(strip, other)

                @pl.when(edge_from != gy)
                def _():
                    hello(edge_from, other)

                hello(chip + 1 - core, gz)

    lane = lax.broadcasted_iota(jnp.int32, (16, 128), 1)
    row = lax.broadcasted_iota(jnp.int32, (16, 128), 0)
    blk = lane // 16
    win = lax.rem(lane, 16)

    for copy in fetch:
        copy.wait()

    def pack_field(a):
        planes = []
        for z in range(8):
            v = v_ref[z]
            mat = mat_ref[z]
            if a == 0:
                f = v
            elif a == 1:
                f = jnp.where(mat == 0, 1.0, jnp.where(mat == 1, 0.33, 0.64)).astype(F32)
            else:
                charge = 0.5 * imp_ref[z].astype(F32) - 1.5
                f = jnp.where(mat == 0, jnp.exp(v) - jnp.exp(-v) - charge, 0.0)
            planes.append(f)
        for j in range(TILES):
            out = roll_l(planes[7], 16 * 7 - WIDE * j + 3)
            for z in range(7):
                out = jnp.where(blk == z, roll_l(planes[z], 16 * z - WIDE * j + 3), out)
            pack[j, a] = out

    for a in range(3):
        pack_field(a)

    pl.semaphore_wait(barrier, 4 * TILES)

    def copy_of(part, j, rows, device, send, got):
        a, n = FIELDS[part]
        src, dst, count = rows
        return pltpu.make_async_remote_copy(
            src_ref=pack.at[j, pl.ds(a, n), pl.ds(src, count)],
            dst_ref=recv.at[gz // 4, lax.rem(gz, 4), pl.ds(a, n), pl.ds(dst, count)],
            send_sem=send,
            recv_sem=got,
            device_id=device,
            device_id_type=MESH,
        )

    def main_copy(part, k, to_core):
        j = lax.rem(tile + k, TILES)
        return copy_of(
            part, j, MAIN[to_core], (chip + to_core, owner_place(2 * j + core)),
            main_send.at[part, to_core, k], main_recv.at[part, gz],
        )

    def edge_copy(part, k, upper):
        j = lax.rem(tile + k, TILES)
        to = lax.rem(gy + core + (GYS - 1 if upper else 0), GYS)
        return copy_of(
            part, j, (UPPER if upper else LOWER)[part], (to, owner_place(2 * j + 1 - core)),
            edge_send.at[part, upper, k], edge_recv.at[part, gz],
        )

    def keep(part, rows, got):
        a, n = FIELDS[part]
        src, dst, count = rows
        pltpu.make_async_copy(
            pack.at[tile, pl.ds(a, n), pl.ds(src, count)],
            recv.at[gz // 4, lax.rem(gz, 4), pl.ds(a, n), pl.ds(dst, count)],
            got.at[part, gz],
        ).start()

    main_self = [owner & (par == core) & (core == to_core) for to_core in (0, 1)]
    edge_self = [owner & (core == 0) & (par == 1), owner & (core == 1) & (par == 0)]

    def start_all(part):
        for k in TILES_FAR_FIRST:
            for w in (0, 1):
                if k:
                    main_copy(part, k, w).start()
                    edge_copy(part, k, w).start()
                else:

                    @pl.when(main_self[w])
                    def _():
                        keep(part, MAIN[w], main_recv)

                    @pl.when(jnp.logical_not(main_self[w]))
                    def _():
                        main_copy(part, k, w).start()

                    @pl.when(edge_self[w])
                    def _():
                        keep(part, (UPPER if w else LOWER)[part], edge_recv)

                    @pl.when(jnp.logical_not(edge_self[w]))
                    def _():
                        edge_copy(part, k, w).start()

    def sent_all(part):
        for k in range(TILES):
            for w in (0, 1):
                if k:
                    main_copy(part, k, w).wait_send()
                    edge_copy(part, k, w).wait_send()
                else:

                    @pl.when(jnp.logical_not(main_self[w]))
                    def _():
                        main_copy(part, k, w).wait_send()

                    @pl.when(jnp.logical_not(edge_self[w]))
                    def _():
                        edge_copy(part, k, w).wait_send()

    slot = core * TILES + tile

    def back_copy(to):
        return pltpu.make_async_remote_copy(
            src_ref=send_back.at[to],
            dst_ref=got_back.at[slot],
            send_sem=back_send.at[to],
            recv_sem=back_recv.at[slot],
            device_id=(strip, to),
            device_id_type=MESH,
        )

    start_all(0)
    sent_all(0)
    start_all(1)

    @pl.when(owner)
    def _():
        y = strip * 16 + core * 8 - 4 + row
        x = tile * WIDE - 3 + win
        inside = (row >= 1) & (row <= 14) & (y >= 0) & (y < GYS * 16) & (x >= 0) & (x < 128)
        odd_cell = lax.rem(row + win, 2) == 1
        inner = inside & (row >= 2) & (row <= 13)
        colour0 = inner & odd_cell
        colour1 = inner & jnp.logical_not(odd_cell)

        def forward_copy(part, q, frm):
            a, n = FIELDS[part]
            src, dst, count = FORWARD[part][frm]
            return pltpu.make_async_remote_copy(
                src_ref=recv.at[:, q, pl.ds(a, n), pl.ds(src, count)],
                dst_ref=recv.at[:, q, pl.ds(a, n), pl.ds(dst, count)],
                send_sem=fwd_send.at[part, q],
                recv_sem=fwd_recv.at[part, q],
                device_id=(chip + 1 - frm, gz),
                device_id_type=MESH,
            )

        def forward(part):
            a, n = FIELDS[part]
            for q in range(4):
                for c in range(8):
                    s = 4 * c + q
                    for count, sem in ((8, main_recv), (LOWER[part][2], edge_recv)):
                        piece = recv.at[0, 0, pl.ds(a, n), pl.ds(4, count)]
                        pltpu.make_async_copy(piece, piece, sem.at[part, s]).wait()
                for frm in (0, 1):

                    @pl.when(core == frm)
                    def _():
                        forward_copy(part, q, frm).start()

        def forwarded(part, q):
            a, n = FIELDS[part]
            piece = recv.at[:, 0, pl.ds(a, n), pl.ds(4, LOWER[part][2])]
            pltpu.make_async_copy(piece, piece, fwd_recv.at[part, q]).wait()

        forward(0)
        for q in range(4):
            forwarded(0, q)
            for a in range(2):
                parts = swap_blocks([recv[c, q, a] for c in range(8)], blk)
                for z in range(8):
                    grid[a, 8 * q + z] = jnp.where(inside, parts[z], 0.0)

        for a in range(2):
            grid[a, 32] = jnp.where(blk == 7, 0.0, roll_l(grid[a, 0], -16))

        k_last = ZW * face(grid[1, 31], grid[1, 32])
        flow_last = k_last * (grid[0, 32] - grid[0, 31])
        k_floor = ZW * grid[1, 0]
        at_floor = blk == 0
        first_link = jnp.where(at_floor, 0.0, roll_l(k_last, 16))
        flow_first = jnp.where(at_floor, k_floor * grid[0, 0], roll_l(flow_last, 16))
        outside_one = jnp.where(inside, 0.0, 1.0)

        def assemble(i, flow_below):
            v = grid[0, i]
            p = grid[1, i]
            kz = ZW * face(p, grid[1, i + 1])
            flow = kz * (grid[0, i + 1] - v)
            px = face(p, roll_l(p, -1))
            py = face(p, roll_r(p, -1))
            flow_x = px * (roll_l(v, -1) - v)
            flow_y = py * (roll_r(v, -1) - v)
            soft = jnp.where(p == 1.0, jnp.exp(v) + jnp.exp(-v), 0.0) + outside_one
            extra = (px + roll_l(px, 1)) + (py + roll_r(py, 1)) + soft
            rhs0[i] = (flow - flow_below) + (flow_x - roll_l(flow_x, 1)) + (flow_y - roll_r(flow_y, 1))
            cond[i] = kz
            excess[i] = extra
            fx[i] = px
            fy[i] = py
            k2 = kz + roll_l(kz, -1)
            ccond[i] = k2 + roll_r(k2, -1)
            e2 = extra + roll_l(extra, -1) - 2.0 * px
            y2 = py + roll_l(py, -1)
            cexcess[i] = e2 + roll_r(e2, -1) - 2.0 * y2
            return flow

        lax.fori_loop(0, 32, assemble, flow_first, unroll=32)

        def quad(f):
            f = f + roll_l(f, -1)
            return f + roll_r(f, -1)

        floor = jnp.where(at_floor, k_floor, 0.0)
        roof = jnp.where(blk == 7, k_last, 0.0)
        excess[0] = excess[0] + floor
        excess[31] = excess[31] + roof
        cexcess[0] = cexcess[0] + quad(floor)
        cexcess[31] = cexcess[31] + quad(roof)

        fine = eliminate(cond, excess, first_link, inv, m, h, blk)
        coarse = eliminate(ccond, cexcess, quad(first_link), cinv, cm, ch, blk)

        forward(1)
        for q in range(4):
            forwarded(1, q)
            parts = swap_blocks([recv[c, q, 2] for c in range(8)], blk)
            for z in range(8):
                force = rhs0[8 * q + z] - parts[z]
                rhs0[8 * q + z] = jnp.where(colour0, force, 0.0)
                rhs1[8 * q + z] = jnp.where(colour1, force, 0.0)

        line_solve(rhs0, fine, inv, m, h, bb, x0)

        def lateral(f, i):
            gx, gyy = fx[i], fy[i]
            return (gx * roll_l(f, -1) + roll_l(gx * f, 1)) + (gyy * roll_r(f, -1) + roll_r(gyy * f, 1))

        def side(i, carry):
            rhs1[i] = jnp.where(colour1, rhs1[i] + lateral(x0[i], i), 0.0)
            return carry

        lax.fori_loop(0, 32, side, 0, unroll=32)
        line_solve(rhs1, fine, inv, m, h, bb, x1)

        def restrict(i, carry):
            rhs0[i] = quad(jnp.where(colour0, lateral(x1[i], i), 0.0))
            return carry

        lax.fori_loop(0, 32, restrict, 0, unroll=32)
        line_solve(rhs0, coarse, cinv, cm, ch, bb, xc)

        odd_x = lax.rem(lane, 2) == 1
        even_y = lax.rem(row, 2) == 0

        for q in range(4):
            parts = []
            for z in range(8):
                i = 8 * q + z
                f = xc[i]
                f = jnp.where(odd_x, f, roll_l(f, 1))
                f = jnp.where(even_y, f, roll_r(f, 1))
                parts.append((x0[i] + x1[i] + f)[4:12])
            for c, f in enumerate(swap_blocks(parts, blk[:8])):
                send_back[4 * c + q] = f


        for k in FAR_FIRST:
            to = lax.rem(gz + k, SEGS)
            if k:
                back_copy(to).start()
            else:

                @pl.when(strip == gy)
                def _():
                    pltpu.make_async_copy(
                        send_back.at[gz], got_back.at[slot], back_recv.at[slot]
                    ).start()

                @pl.when(strip != gy)
                def _():
                    back_copy(to).start()

        for part in (0, 1):
            for q in range(4):
                for frm in (0, 1):

                    @pl.when(core == frm)
                    def _():
                        forward_copy(part, q, frm).wait_send()

    sent_all(1)

    for k in range(OWNERS):
        pltpu.make_async_copy(send_back.at[0], send_back.at[0], back_recv.at[k]).wait()

    column = lane[:8] // WIDE
    for to_core in (0, 1):
        rows = pl.ds(8 * to_core, 8)
        for z in range(8):
            f = roll_l(got_back[to_core * TILES], -3 - 16 * z)
            for j in range(1, TILES):
                f = jnp.where(
                    column == j, roll_l(got_back[to_core * TILES + j], WIDE * j - 3 - 16 * z), f
                )
            o_ref[z, rows] = v_ref[z, rows] + f

    @pl.when(owner)
    def _():
        for k in range(SEGS):
            if k:
                back_copy(lax.rem(gz + k, SEGS)).wait_send()
            else:

                @pl.when(strip != gy)
                def _():
                    back_copy(gz).wait_send()


def body(electric_level, impurity_atoms, cell_materials):
    fields = (electric_level, impurity_atoms, cell_materials)
    line = pltpu.VMEM((32, 16, 128), F32)
    vmem = pl.BlockSpec(memory_space=pltpu.VMEM)
    return pl.pallas_call(
        kernel,
        out_shape=jax.ShapeDtypeStruct(electric_level.shape, F32),
        in_specs=[pl.BlockSpec(memory_space=pltpu.HBM)] * 3,
        out_specs=vmem,
        scratch_shapes=[
            pltpu.VMEM(electric_level.shape, F32),
            pltpu.VMEM(electric_level.shape, jnp.int32),
            pltpu.VMEM(electric_level.shape, jnp.int32),
            pltpu.SemaphoreType.DMA((3,)),
            pltpu.VMEM((TILES, 3, 16, 128), F32),
            pltpu.VMEM((8, 4, 3, 16, 128), F32),
            pltpu.VMEM((SEGS, 8, 128), F32),
            pltpu.VMEM((OWNERS, 8, 128), F32),
            pltpu.VMEM((2, 33, 16, 128), F32),
        ]
        + [line] * 18
        + [pltpu.SemaphoreType.DMA((2, 2, TILES))] * 2
        + [pltpu.SemaphoreType.DMA((2, SEGS))] * 2
        + [pltpu.SemaphoreType.DMA((2, 4))] * 2
        + [pltpu.SemaphoreType.DMA((SEGS,)), pltpu.SemaphoreType.DMA((OWNERS,))],
        compiler_params=pltpu.CompilerParams(
            collective_id=0, has_side_effects=True, vmem_limit_bytes=32 * 1024 * 1024
        ),
        cost_estimate=pl.CostEstimate(flops=20_000_000, bytes_accessed=262144, transcendentals=200_000),
        name="newton_step",
    )(*(pltpu.with_memory_space_constraint(f, pltpu.HBM) for f in fields))


def solution(mesh):
    placed = P("gz", "gy", None)
    return jax.shard_map(
        body, mesh=mesh, in_specs=(placed,) * 3, out_specs=placed, check_vma=False
    )
```

time: 46 us -> 46.6 us (1.013)
  Pallas kernels: 45.2 us -> 45.8 us
    pallas_call x1, Pallas kernels: 45.2 us -> 45.8 us  [body(): pl.pallas_call(kernel, out_shape=jax.ShapeDtypeStruct(electric_level.shap...]
where the time goes in v4:
time: 46.6 us; the launch traced here: 46.5 us
  Pallas kernels  45.8 us (98%)
  local copies, waits for them, and re-layouts  0.63 us (1%)
    pallas_call x1, Pallas kernels, body(): pl.pallas_call(kernel, out_shape=jax.ShapeDtypeStruct(electric_level.shap...  45.8 us

profile of v4, /device:TPU:1, one launch (start us, length us, event | category | flops | bytes accessed | tf_op | source)
XLA Modules:
  0.0 46.5 jit_solution(8068450884871586798)
XLA Ops:
  0.0 45.8 %newton_step.1 = f32[8,16,128]{2,1,0:T(8,128)S(1)} custom-call(f32[8,16,128]{2,1,0:T(8,128)} %v_hbm.1, s32[8,16,128]{2,1,0:T(8,128)} %imp_hbm.1, s32[8,16,128]{2,1,0:T(8,128)} %mat_hbm.1), custom_call_target="tpu_custom_call" | custom-call | flops 20000000 | bytes 262144 | tf_op jit(solution)/shard_map/newton_step/pallas_call | solution.py:529
  45.8 0.6 %copy.5 = f32[8,16,128]{2,1,0:T(8,128)} copy(f32[8,16,128]{2,1,0:T(8,128)S(1)} %newton_step.1) | data formatting | bytes 131072

commit v5 on v4

--- a/solution.py
+++ b/solution.py
@@ -54,10 +54,10 @@
     return jnp.where(prod > 0, 2.0 * prod / total, total)
 
 
-MAIN = ((0, 4, 8), (8, 4, 8))
-LOWER = ((13, 1, 3), (14, 2, 2))
-UPPER = ((0, 12, 3), (0, 12, 2))
-FORWARD = (((9, 1, 3), (4, 12, 3)), ((10, 2, 2), (4, 12, 2)))
+MAIN = ((0, 0, 8), (8, 0, 8))
+LOWER = ((13, 13, 3), (14, 14, 2))
+UPPER = ((0, 8, 3), (0, 8, 2))
+FORWARD = (((5, 13, 3), (0, 8, 3)), ((6, 14, 2), (0, 8, 2)))
 FIELDS = ((0, 2), (2, 1))
 
 
@@ -156,8 +156,8 @@
 def kernel(
     v_hbm, imp_hbm, mat_hbm, o_ref,
     v_ref, imp_ref, mat_ref, in_sem, pack, recv, send_back, got_back, grid,
-    cond, excess, rhs0, rhs1, fx, fy, ccond, cexcess, inv, m, h, cinv, cm, ch, bb, x0, x1, xc,
-    main_send, edge_send, main_recv, edge_recv, fwd_send, fwd_recv, back_send, back_recv,
+    cond, excess, rhs0, rhs1, fx, fy, ccond, cexcess, inv, m, h, cinv, cm, ch, bb, x0, x1, xc, crhs, cbb,
+    main_send, edge_send, arrived, fwd_send, fwd_recv, back_send, back_recv,
 ):
     gy, gz = lax.axis_index("gy"), lax.axis_index("gz")
     core = lax.rem(gy, 2)
@@ -248,7 +248,7 @@
         j = lax.rem(tile + k, TILES)
         return copy_of(
             part, j, MAIN[to_core], (chip + to_core, owner_place(2 * j + core)),
-            main_send.at[part, to_core, k], main_recv.at[part, gz],
+            main_send.at[part, to_core, k], arrived.at[part, lax.rem(gz, 4)],
         )
 
     def edge_copy(part, k, upper):
@@ -256,16 +256,16 @@
         to = lax.rem(gy + core + (GYS - 1 if upper else 0), GYS)
         return copy_of(
             part, j, (UPPER if upper else LOWER)[part], (to, owner_place(2 * j + 1 - core)),
-            edge_send.at[part, upper, k], edge_recv.at[part, gz],
+            edge_send.at[part, upper, k], arrived.at[part, lax.rem(gz, 4)],
         )
 
-    def keep(part, rows, got):
+    def keep(part, rows):
         a, n = FIELDS[part]
         src, dst, count = rows
         pltpu.make_async_copy(
             pack.at[tile, pl.ds(a, n), pl.ds(src, count)],
             recv.at[gz // 4, lax.rem(gz, 4), pl.ds(a, n), pl.ds(dst, count)],
-            got.at[part, gz],
+            arrived.at[part, lax.rem(gz, 4)],
         ).start()
 
     main_self = [owner & (par == core) & (core == to_core) for to_core in (0, 1)]
@@ -281,7 +281,7 @@
 
                     @pl.when(main_self[w])
                     def _():
-                        keep(part, MAIN[w], main_recv)
+                        keep(part, MAIN[w])
 
                     @pl.when(jnp.logical_not(main_self[w]))
                     def _():
@@ -289,7 +289,7 @@
 
                     @pl.when(edge_self[w])
                     def _():
-                        keep(part, (UPPER if w else LOWER)[part], edge_recv)
+                        keep(part, (UPPER if w else LOWER)[part])
 
                     @pl.when(jnp.logical_not(edge_self[w]))
                     def _():
@@ -318,7 +318,7 @@
             src_ref=send_back.at[to],
             dst_ref=got_back.at[slot],
             send_sem=back_send.at[to],
-            recv_sem=back_recv.at[slot],
+            recv_sem=back_recv.at[0],
             device_id=(strip, to),
             device_id_type=MESH,
         )
@@ -329,11 +329,11 @@
 
     @pl.when(owner)
     def _():
-        y = strip * 16 + core * 8 - 4 + row
+        y = strip * 16 + core * 8 + jnp.where(row < 12, row, row - 16)
         x = tile * WIDE - 3 + win
-        inside = (row >= 1) & (row <= 14) & (y >= 0) & (y < GYS * 16) & (x >= 0) & (x < 128)
+        inside = ((row <= 10) | (row >= 13)) & (y >= 0) & (y < GYS * 16) & (x >= 0) & (x < 128)
         odd_cell = lax.rem(row + win, 2) == 1
-        inner = inside & (row >= 2) & (row <= 13)
+        inner = inside & ((row <= 9) | (row >= 14))
         colour0 = inner & odd_cell
         colour1 = inner & jnp.logical_not(odd_cell)
 
@@ -352,11 +352,8 @@
         def forward(part):
             a, n = FIELDS[part]
             for q in range(4):
-                for c in range(8):
-                    s = 4 * c + q
-                    for count, sem in ((8, main_recv), (LOWER[part][2], edge_recv)):
-                        piece = recv.at[0, 0, pl.ds(a, n), pl.ds(4, count)]
-                        pltpu.make_async_copy(piece, piece, sem.at[part, s]).wait()
+                piece = recv.at[:, q, pl.ds(a, n), pl.ds(0, 8 + LOWER[part][2])]
+                pltpu.make_async_copy(piece, piece, arrived.at[part, q]).wait()
                 for frm in (0, 1):
 
                     @pl.when(core == frm)
@@ -365,7 +362,7 @@
 
         def forwarded(part, q):
             a, n = FIELDS[part]
-            piece = recv.at[:, 0, pl.ds(a, n), pl.ds(4, LOWER[part][2])]
+            piece = recv.at[:, 0, pl.ds(a, n), pl.ds(0, LOWER[part][2])]
             pltpu.make_async_copy(piece, piece, fwd_recv.at[part, q]).wait()
 
         forward(0)
@@ -386,6 +383,10 @@
         first_link = jnp.where(at_floor, 0.0, roll_l(k_last, 16))
         flow_first = jnp.where(at_floor, k_floor * grid[0, 0], roll_l(flow_last, 16))
         outside_one = jnp.where(inside, 0.0, 1.0)
+
+        def quad(f):
+            f = f + roll_l(f, -1)
+            return f + pltpu.roll(f, 7, 0)
 
         def assemble(i, flow_below):
             v = grid[0, i]
@@ -403,28 +404,23 @@
             excess[i] = extra
             fx[i] = px
             fy[i] = py
-            k2 = kz + roll_l(kz, -1)
-            ccond[i] = k2 + roll_r(k2, -1)
-            e2 = extra + roll_l(extra, -1) - 2.0 * px
-            y2 = py + roll_l(py, -1)
-            cexcess[i] = e2 + roll_r(e2, -1) - 2.0 * y2
+            ccond[i] = quad(kz[:8])
+            e2 = extra[:8] + roll_l(extra[:8], -1) - 2.0 * px[:8]
+            y2 = py[:8] + roll_l(py[:8], -1)
+            cexcess[i] = e2 + pltpu.roll(e2, 7, 0) - 2.0 * y2
             return flow
 
         lax.fori_loop(0, 32, assemble, flow_first, unroll=32)
-
-        def quad(f):
-            f = f + roll_l(f, -1)
-            return f + roll_r(f, -1)
 
         floor = jnp.where(at_floor, k_floor, 0.0)
         roof = jnp.where(blk == 7, k_last, 0.0)
         excess[0] = excess[0] + floor
         excess[31] = excess[31] + roof
-        cexcess[0] = cexcess[0] + quad(floor)
-        cexcess[31] = cexcess[31] + quad(roof)
+        cexcess[0] = cexcess[0] + quad(floor[:8])
+        cexcess[31] = cexcess[31] + quad(roof[:8])
 
         fine = eliminate(cond, excess, first_link, inv, m, h, blk)
-        coarse = eliminate(ccond, cexcess, quad(first_link), cinv, cm, ch, blk)
+        coarse = eliminate(ccond, cexcess, quad(first_link[:8]), cinv, cm, ch, blk)
 
         forward(1)
         for q in range(4):
@@ -449,11 +445,17 @@
         line_solve(rhs1, fine, inv, m, h, bb, x1)
 
         def restrict(i, carry):
-            rhs0[i] = quad(jnp.where(colour0, lateral(x1[i], i), 0.0))
+            f = x1[i]
+            g = fy[i] * f
+            gx, gyy, t = fx[i, :8], fy[i, :8], f[:8]
+            out = (gx * roll_l(t, -1) + roll_l(gx * t, 1)) + (
+                gyy * roll_r(f, -1)[:8] + roll_r(g, 1)[:8]
+            )
+            crhs[i] = quad(jnp.where(colour0[:8], out, 0.0))
             return carry
 
         lax.fori_loop(0, 32, restrict, 0, unroll=32)
-        line_solve(rhs0, coarse, cinv, cm, ch, bb, xc)
+        line_solve(crhs, coarse, cinv, cm, ch, cbb, xc)
 
         odd_x = lax.rem(lane, 2) == 1
         even_y = lax.rem(row, 2) == 0
@@ -463,9 +465,9 @@
             for z in range(8):
                 i = 8 * q + z
                 f = xc[i]
-                f = jnp.where(odd_x, f, roll_l(f, 1))
-                f = jnp.where(even_y, f, roll_r(f, 1))
-                parts.append((x0[i] + x1[i] + f)[4:12])
+                f = jnp.where(odd_x[:8], f, roll_l(f, 1))
+                f = jnp.where(even_y[:8], f, pltpu.roll(f, 1, 0))
+                parts.append(x0[i, :8] + x1[i, :8] + f)
             for c, f in enumerate(swap_blocks(parts, blk[:8])):
                 send_back[4 * c + q] = f
 
@@ -479,7 +481,7 @@
                 @pl.when(strip == gy)
                 def _():
                     pltpu.make_async_copy(
-                        send_back.at[gz], got_back.at[slot], back_recv.at[slot]
+                        send_back.at[gz], got_back.at[slot], back_recv.at[0]
                     ).start()
 
                 @pl.when(strip != gy)
@@ -496,8 +498,7 @@
 
     sent_all(1)
 
-    for k in range(OWNERS):
-        pltpu.make_async_copy(send_back.at[0], send_back.at[0], back_recv.at[k]).wait()
+    pltpu.make_async_copy(got_back, got_back, back_recv.at[0]).wait()
 
     column = lane[:8] // WIDE
     for to_core in (0, 1):
@@ -525,6 +526,7 @@
 def body(electric_level, impurity_atoms, cell_materials):
     fields = (electric_level, impurity_atoms, cell_materials)
     line = pltpu.VMEM((32, 16, 128), F32)
+    half = pltpu.VMEM((32, 8, 128), F32)
     vmem = pl.BlockSpec(memory_space=pltpu.VMEM)
     return pl.pallas_call(
         kernel,
@@ -542,11 +544,15 @@
             pltpu.VMEM((OWNERS, 8, 128), F32),
             pltpu.VMEM((2, 33, 16, 128), F32),
         ]
-        + [line] * 18
+        + [line] * 6
+        + [half] * 2
+        + [line] * 3
+        + [half] * 3
+        + [line] * 3
+        + [half] * 3
         + [pltpu.SemaphoreType.DMA((2, 2, TILES))] * 2
-        + [pltpu.SemaphoreType.DMA((2, SEGS))] * 2
-        + [pltpu.SemaphoreType.DMA((2, 4))] * 2
-        + [pltpu.SemaphoreType.DMA((SEGS,)), pltpu.SemaphoreType.DMA((OWNERS,))],
+        + [pltpu.SemaphoreType.DMA((2, 4))] * 3
+        + [pltpu.SemaphoreType.DMA((SEGS,)), pltpu.SemaphoreType.DMA((1,))],
         compiler_params=pltpu.CompilerParams(
             collective_id=0, has_side_effects=True, vmem_limit_bytes=32 * 1024 * 1024
         ),

time: 46.6 us -> 44.3 us (0.951)
  Pallas kernels: 45.8 us -> 43.5 us
    pallas_call x1, Pallas kernels: 45.8 us -> 43.5 us  [body(): pl.pallas_call(kernel, out_shape=jax.ShapeDtypeStruct(electric_level.shap...]
where the time goes in v5:
time: 44.3 us; the launch traced here: 44.1 us
  Pallas kernels  43.5 us (98%)
  local copies, waits for them, and re-layouts  0.63 us (1%)
    pallas_call x1, Pallas kernels, body(): pl.pallas_call(kernel, out_shape=jax.ShapeDtypeStruct(electric_level.shap...  43.5 us

profile of v5, /device:TPU:1, one launch (start us, length us, event | category | flops | bytes accessed | tf_op | source)
XLA Modules:
  0.0 44.1 jit_solution(5136013037347689223)
XLA Ops:
  0.0 43.5 %newton_step.1 = f32[8,16,128]{2,1,0:T(8,128)S(1)} custom-call(f32[8,16,128]{2,1,0:T(8,128)} %v_hbm.1, s32[8,16,128]{2,1,0:T(8,128)} %imp_hbm.1, s32[8,16,128]{2,1,0:T(8,128)} %mat_hbm.1), custom_call_target="tpu_custom_call" | custom-call | flops 20000000 | bytes 262144 | tf_op jit(solution)/shard_map/newton_step/pallas_call | solution.py:531
  43.5 0.6 %copy.5 = f32[8,16,128]{2,1,0:T(8,128)} copy(f32[8,16,128]{2,1,0:T(8,128)S(1)} %newton_step.1) | data formatting | bytes 131072

commit v6 on v5

--- a/solution.py
+++ b/solution.py
@@ -29,7 +29,7 @@
 
 
 def roll_l(v, s):
-    return pltpu.roll(v, s % 128, 1)
+    return pltpu.roll(v, s % 128, 1) if s % 128 else v
 
 
 def roll_r(v, s):
@@ -54,10 +54,12 @@
     return jnp.where(prod > 0, 2.0 * prod / total, total)
 
 
-MAIN = ((0, 0, 8), (8, 0, 8))
+MAIN = (((0, 0, 8), (8, 0, 8)), ((0, 0, 10), (8, 0, 8)))
+INNER = (6, 14, 2)
 LOWER = ((13, 13, 3), (14, 14, 2))
 UPPER = ((0, 8, 3), (0, 8, 2))
-FORWARD = (((5, 13, 3), (0, 8, 3)), ((6, 14, 2), (0, 8, 2)))
+FORWARD = ((5, 13, 3), (0, 8, 3))
+ROWS = (11, 12)
 FIELDS = ((0, 2), (2, 1))
 
 
@@ -110,13 +112,35 @@
             alpha * roll_l(low, s),
             beta * roll_l(up, -s),
         )
-        factors.append((s, alpha, beta))
-    return factors, 1.0 / ground
+        factors.append((alpha, beta))
+    (a1, b1), (a2, b2), (a4, b4) = factors
+    one = jnp.ones_like(low)
+    sums = [
+        one,
+        a1 + a2 * roll_l(b1, 32),
+        a2,
+        a2 * roll_l(a1, 32),
+        jnp.zeros_like(low),
+        b2 * roll_l(b1, -32),
+        b2,
+        b1 + b2 * roll_l(a1, -32),
+    ]
+    half = a4 + b4
+    inv = 1.0 / ground
+    own = [inv * (sums[k] + half * roll_l(sums[(k + 4) % 8], 64)) for k in range(8)]
+    before = [roll_l(own[(k + 7) % 8], 16) for k in range(8)]
+    return own, before
+
+
+def total(terms):
+    while len(terms) > 1:
+        terms = [a + b for a, b in zip(terms[::2], terms[1::2])]
+    return terms[0]
 
 
 def line_solve(rhs, factors, inv_ref, m_ref, h_ref, b_ref, x_ref):
-    seps, inv_sep = factors
-    zero = jnp.zeros_like(inv_sep)
+    own, before = factors
+    zero = jnp.zeros_like(own[0])
 
     def forward(i, carry):
         in_a, b_l, in_b, b_r = carry
@@ -131,11 +155,10 @@
     mid = rhs[15] + in_a + in_b
     b_l = b_l + h_ref[15] * mid
     b_r = b_r + m_ref[15] * mid
-    b = rhs[31] + b_r + roll_l(b_l, -16)
-    for s, alpha, beta in seps:
-        b = b + alpha * roll_l(b, s) + beta * roll_l(b, -s)
-    x_r = b * inv_sep
-    x_l = roll_l(x_r, 16)
+    b = rhs[31] + b_r
+    turns = [roll_l(b, 16 * k) + roll_l(b_l, 16 * k - 16) for k in range(8)]
+    x_r = total([f * t for f, t in zip(own, turns)])
+    x_l = total([f * t for f, t in zip(before, turns)])
     x_ref[31] = x_r
     mid = inv_ref[15] * mid + h_ref[15] * x_l + m_ref[15] * x_r
     x_ref[15] = mid
@@ -157,7 +180,7 @@
     v_hbm, imp_hbm, mat_hbm, o_ref,
     v_ref, imp_ref, mat_ref, in_sem, pack, recv, send_back, got_back, grid,
     cond, excess, rhs0, rhs1, fx, fy, ccond, cexcess, inv, m, h, cinv, cm, ch, bb, x0, x1, xc, crhs, cbb,
-    main_send, edge_send, arrived, fwd_send, fwd_recv, back_send, back_recv,
+    main_send, edge_send, inner_send, arrived, fwd_send, fwd_recv, back_send, back_recv,
 ):
     gy, gz = lax.axis_index("gy"), lax.axis_index("gz")
     core = lax.rem(gy, 2)
@@ -247,8 +270,15 @@
     def main_copy(part, k, to_core):
         j = lax.rem(tile + k, TILES)
         return copy_of(
-            part, j, MAIN[to_core], (chip + to_core, owner_place(2 * j + core)),
+            part, j, MAIN[part][to_core], (chip + to_core, owner_place(2 * j + core)),
             main_send.at[part, to_core, k], arrived.at[part, lax.rem(gz, 4)],
+        )
+
+    def inner_copy(k):
+        j = lax.rem(tile + k, TILES)
+        return copy_of(
+            1, j, INNER, (chip + 1, owner_place(2 * j + core)),
+            inner_send.at[k], arrived.at[1, lax.rem(gz, 4)],
         )
 
     def edge_copy(part, k, upper):
@@ -277,15 +307,21 @@
                 if k:
                     main_copy(part, k, w).start()
                     edge_copy(part, k, w).start()
+                    if part and w:
+                        inner_copy(k).start()
                 else:
 
                     @pl.when(main_self[w])
                     def _():
-                        keep(part, MAIN[w])
+                        keep(part, MAIN[part][w])
+                        if part and w:
+                            keep(part, INNER)
 
                     @pl.when(jnp.logical_not(main_self[w]))
                     def _():
                         main_copy(part, k, w).start()
+                        if part and w:
+                            inner_copy(k).start()
 
                     @pl.when(edge_self[w])
                     def _():
@@ -301,11 +337,15 @@
                 if k:
                     main_copy(part, k, w).wait_send()
                     edge_copy(part, k, w).wait_send()
+                    if part and w:
+                        inner_copy(k).wait_send()
                 else:
 
                     @pl.when(jnp.logical_not(main_self[w]))
                     def _():
                         main_copy(part, k, w).wait_send()
+                        if part and w:
+                            inner_copy(k).wait_send()
 
                     @pl.when(jnp.logical_not(edge_self[w]))
                     def _():
@@ -318,7 +358,7 @@
             src_ref=send_back.at[to],
             dst_ref=got_back.at[slot],
             send_sem=back_send.at[to],
-            recv_sem=back_recv.at[0],
+            recv_sem=back_recv.at[core],
             device_id=(strip, to),
             device_id_type=MESH,
         )
@@ -337,37 +377,33 @@
         colour0 = inner & odd_cell
         colour1 = inner & jnp.logical_not(odd_cell)
 
-        def forward_copy(part, q, frm):
-            a, n = FIELDS[part]
-            src, dst, count = FORWARD[part][frm]
+        def forward_copy(q, frm):
+            src, dst, count = FORWARD[frm]
             return pltpu.make_async_remote_copy(
-                src_ref=recv.at[:, q, pl.ds(a, n), pl.ds(src, count)],
-                dst_ref=recv.at[:, q, pl.ds(a, n), pl.ds(dst, count)],
-                send_sem=fwd_send.at[part, q],
-                recv_sem=fwd_recv.at[part, q],
+                src_ref=recv.at[:, q, pl.ds(0, 2), pl.ds(src, count)],
+                dst_ref=recv.at[:, q, pl.ds(0, 2), pl.ds(dst, count)],
+                send_sem=fwd_send.at[q],
+                recv_sem=fwd_recv.at[q],
                 device_id=(chip + 1 - frm, gz),
                 device_id_type=MESH,
             )
 
-        def forward(part):
+        def landed(part, q):
             a, n = FIELDS[part]
-            for q in range(4):
-                piece = recv.at[:, q, pl.ds(a, n), pl.ds(0, 8 + LOWER[part][2])]
-                pltpu.make_async_copy(piece, piece, arrived.at[part, q]).wait()
-                for frm in (0, 1):
-
-                    @pl.when(core == frm)
-                    def _():
-                        forward_copy(part, q, frm).start()
-
-        def forwarded(part, q):
-            a, n = FIELDS[part]
-            piece = recv.at[:, 0, pl.ds(a, n), pl.ds(0, LOWER[part][2])]
-            pltpu.make_async_copy(piece, piece, fwd_recv.at[part, q]).wait()
-
-        forward(0)
+            piece = recv.at[:, q, pl.ds(a, n), pl.ds(0, ROWS[part])]
+            pltpu.make_async_copy(piece, piece, arrived.at[part, q]).wait()
+
         for q in range(4):
-            forwarded(0, q)
+            landed(0, q)
+            for frm in (0, 1):
+
+                @pl.when(core == frm)
+                def _():
+                    forward_copy(q, frm).start()
+
+        for q in range(4):
+            piece = recv.at[:, q, pl.ds(0, 2), pl.ds(0, 3)]
+            pltpu.make_async_copy(piece, piece, fwd_recv.at[q]).wait()
             for a in range(2):
                 parts = swap_blocks([recv[c, q, a] for c in range(8)], blk)
                 for z in range(8):
@@ -422,9 +458,8 @@
         fine = eliminate(cond, excess, first_link, inv, m, h, blk)
         coarse = eliminate(ccond, cexcess, quad(first_link[:8]), cinv, cm, ch, blk)
 
-        forward(1)
         for q in range(4):
-            forwarded(1, q)
+            landed(1, q)
             parts = swap_blocks([recv[c, q, 2] for c in range(8)], blk)
             for z in range(8):
                 force = rhs0[8 * q + z] - parts[z]
@@ -481,28 +516,28 @@
                 @pl.when(strip == gy)
                 def _():
                     pltpu.make_async_copy(
-                        send_back.at[gz], got_back.at[slot], back_recv.at[0]
+                        send_back.at[gz], got_back.at[slot], back_recv.at[core]
                     ).start()
 
                 @pl.when(strip != gy)
                 def _():
                     back_copy(to).start()
 
-        for part in (0, 1):
-            for q in range(4):
-                for frm in (0, 1):
-
-                    @pl.when(core == frm)
-                    def _():
-                        forward_copy(part, q, frm).wait_send()
+        for q in range(4):
+            for frm in (0, 1):
+
+                @pl.when(core == frm)
+                def _():
+                    forward_copy(q, frm).wait_send()
 
     sent_all(1)
 
-    pltpu.make_async_copy(got_back, got_back, back_recv.at[0]).wait()
 
     column = lane[:8] // WIDE
     for to_core in (0, 1):
         rows = pl.ds(8 * to_core, 8)
+        piece = got_back.at[pl.ds(to_core * TILES, TILES)]
+        pltpu.make_async_copy(piece, piece, back_recv.at[to_core]).wait()
         for z in range(8):
             f = roll_l(got_back[to_core * TILES], -3 - 16 * z)
             for j in range(1, TILES):
@@ -551,8 +586,9 @@
         + [line] * 3
         + [half] * 3
         + [pltpu.SemaphoreType.DMA((2, 2, TILES))] * 2
-        + [pltpu.SemaphoreType.DMA((2, 4))] * 3
-        + [pltpu.SemaphoreType.DMA((SEGS,)), pltpu.SemaphoreType.DMA((1,))],
+        + [pltpu.SemaphoreType.DMA((TILES,)), pltpu.SemaphoreType.DMA((2, 4))]
+        + [pltpu.SemaphoreType.DMA((4,))] * 2
+        + [pltpu.SemaphoreType.DMA((SEGS,)), pltpu.SemaphoreType.DMA((2,))],
         compiler_params=pltpu.CompilerParams(
             collective_id=0, has_side_effects=True, vmem_limit_bytes=32 * 1024 * 1024
         ),

time: 44.3 us -> 43.4 us (0.980)
  Pallas kernels: 43.5 us -> 42.6 us
    pallas_call x1, Pallas kernels: 43.5 us -> 42.6 us  [body(): pl.pallas_call(kernel, out_shape=jax.ShapeDtypeStruct(electric_level.shap...]
where the time goes in v6:
time: 43.4 us; the launch traced here: 43.2 us
  Pallas kernels  42.6 us (98%)
  local copies, waits for them, and re-layouts  0.63 us (1%)
    pallas_call x1, Pallas kernels, body(): pl.pallas_call(kernel, out_shape=jax.ShapeDtypeStruct(electric_level.shap...  42.6 us

profile of v6, /device:TPU:1, one launch (start us, length us, event | category | flops | bytes accessed | tf_op | source)
XLA Modules:
  0.0 43.2 jit_solution(3934470815531441476)
XLA Ops:
  0.0 42.6 %newton_step.1 = f32[8,16,128]{2,1,0:T(8,128)S(1)} custom-call(f32[8,16,128]{2,1,0:T(8,128)} %v_hbm.1, s32[8,16,128]{2,1,0:T(8,128)} %imp_hbm.1, s32[8,16,128]{2,1,0:T(8,128)} %mat_hbm.1), custom_call_target="tpu_custom_call" | custom-call | flops 20000000 | bytes 262144 | tf_op jit(solution)/shard_map/newton_step/pallas_call | solution.py:566
  42.6 0.6 %copy.5 = f32[8,16,128]{2,1,0:T(8,128)} copy(f32[8,16,128]{2,1,0:T(8,128)S(1)} %newton_step.1) | data formatting | bytes 131072

commit v7 on v6

--- a/solution.py
+++ b/solution.py
@@ -25,7 +25,7 @@
 
 
 def owner_place(n):
-    return (16 * n) // TILES
+    return 8 * (n % 4) + n // 4
 
 
 def roll_l(v, s):
@@ -184,8 +184,8 @@
 ):
     gy, gz = lax.axis_index("gy"), lax.axis_index("gz")
     core = lax.rem(gy, 2)
-    number = (TILES * gz + 15) // 16
-    owner = (number < OWNERS) & (owner_place(number) == gz)
+    number = 4 * lax.rem(gz, 8) + gz // 8
+    owner = number < OWNERS
     par, tile = lax.rem(number, 2), lax.rem(number // 2, TILES)
     chip = gy - core
     strip = chip + par

time: 43.4 us -> 41.4 us (0.954)
  Pallas kernels: 42.6 us -> 40.6 us
    pallas_call x1, Pallas kernels: 42.6 us -> 40.6 us  [body(): pl.pallas_call(kernel, out_shape=jax.ShapeDtypeStruct(electric_level.shap...]
where the time goes in v7:
time: 41.4 us; the launch traced here: 41.2 us
  Pallas kernels  40.6 us (98%)
  local copies, waits for them, and re-layouts  0.63 us (2%)
    pallas_call x1, Pallas kernels, body(): pl.pallas_call(kernel, out_shape=jax.ShapeDtypeStruct(electric_level.shap...  40.6 us

profile of v7, /device:TPU:1, one launch (start us, length us, event | category | flops | bytes accessed | tf_op | source)
XLA Modules:
  0.0 41.2 jit_solution(9308338011291560140)
XLA Ops:
  0.0 40.6 %newton_step.1 = f32[8,16,128]{2,1,0:T(8,128)S(1)} custom-call(f32[8,16,128]{2,1,0:T(8,128)} %v_hbm.1, s32[8,16,128]{2,1,0:T(8,128)} %imp_hbm.1, s32[8,16,128]{2,1,0:T(8,128)} %mat_hbm.1), custom_call_target="tpu_custom_call" | custom-call | flops 20000000 | bytes 262144 | tf_op jit(solution)/shard_map/newton_step/pallas_call | solution.py:566
  40.6 0.6 %copy.5 = f32[8,16,128]{2,1,0:T(8,128)} copy(f32[8,16,128]{2,1,0:T(8,128)S(1)} %newton_step.1) | data formatting | bytes 131072

commit v8 on v7

--- a/solution.py
+++ b/solution.py
@@ -21,7 +21,7 @@
 WIDE = 10
 TILES = 13
 OWNERS = 2 * TILES
-TILES_FAR_FIRST = sorted(range(TILES), key=lambda k: -hops((SEGS * k // TILES) % SEGS))
+TILES_FAR_FIRST = sorted(range(TILES), key=lambda k: -hops(16 * (k % 2) + k // 2))
 
 
 def owner_place(n):

time: 41.4 us -> 40.8 us (0.986)
  Pallas kernels: 40.6 us -> 40 us
    pallas_call x1, Pallas kernels: 40.6 us -> 40 us  [body(): pl.pallas_call(kernel, out_shape=jax.ShapeDtypeStruct(electric_level.shap...]
where the time goes in v8:
time: 40.8 us; the launch traced here: 40.6 us
  Pallas kernels  40 us (98%)
  local copies, waits for them, and re-layouts  0.63 us (2%)
    pallas_call x1, Pallas kernels, body(): pl.pallas_call(kernel, out_shape=jax.ShapeDtypeStruct(electric_level.shap...  40 us

profile of v8, /device:TPU:1, one launch (start us, length us, event | category | flops | bytes accessed | tf_op | source)
XLA Modules:
  0.0 40.6 jit_solution(12173535144653537649)
XLA Ops:
  0.0 40.0 %newton_step.1 = f32[8,16,128]{2,1,0:T(8,128)S(1)} custom-call(f32[8,16,128]{2,1,0:T(8,128)} %v_hbm.1, s32[8,16,128]{2,1,0:T(8,128)} %imp_hbm.1, s32[8,16,128]{2,1,0:T(8,128)} %mat_hbm.1), custom_call_target="tpu_custom_call" | custom-call | flops 20000000 | bytes 262144 | tf_op jit(solution)/shard_map/newton_step/pallas_call | solution.py:566
  40.0 0.6 %copy.5 = f32[8,16,128]{2,1,0:T(8,128)} copy(f32[8,16,128]{2,1,0:T(8,128)S(1)} %newton_step.1) | data formatting | bytes 131072
